TPU v7x, 32 devices: a whole 2x2x4 slice. The times are simulated.
32 devices in a mesh: row: 8 (over y, x, core), col: 4 (over z).
Axes of the slice: x: 2, y: 2, z: 4, core: 2. Of those that a mesh axis runs over, the one named last changes fastest.
Arguments:
- values: float32 [8, 4, 36, 128, 128], P('row', 'col'), as said below
- block_ids: int32 [8, 4, 36, 2], P('row', 'col'), may hold values from -1 to 63, as said below
- coupled_rows: int32 [8, 4], replicated, may hold values from 0 to 63, as said below
Outputs:
- factored: float32 [8, 4, 36, 128, 128], P('row', 'col')
Inputs may be any that keep to these rules, and one draw needn't show every extreme that they name: `coupled_rows`: row r holds 4 distinct block rows in increasing order, each equal to r modulo 8; every block row below 4 is among them. `block_ids`: the slots of device (r, c), in an order drawn from the seed, name each block (i, j) with i in row r of coupled_rows, j in a row r2 of coupled_rows with r2 equal to c modulo 4, and j <= i; and each diagonal block (i, i) of a block row i equal to r modulo 8 and to c modulo 4 that is not coupled; every other slot holds (-1, -1). No block is named twice. `values`: every stored diagonal block is symmetric, and the blocks of A in block rows and block columns below 4 form a symmetric positive definite matrix.
All inputs are finite; a program needn't handle non-finite values.
Results may differ from a plain program's by a relative error of at most 0.0003.
Values sent between devices are 32-bit elements; how exact they have to be, the bound alone decides.
No kernel may reach another device: no remote copies, remote signals or barrier semaphores. Data moves between devices by JAX's collectives and lax.ppermute only.
A program may use at most 128 MiB of HBM per device.

v0:
```python
import jax
import jax.numpy as jnp
from jax import lax
from jax.sharding import PartitionSpec as P

PANELS = 4


exact_precision = lax.Precision.HIGHEST


def broadcast(shard, axis, root):
    mine = lax.axis_index(axis) == root
    return lax.psum(jnp.where(mine, shard, jnp.zeros_like(shard)), axis)


def lookup(wanted, known_rows):
    matched = wanted[:, None] == known_rows[None, :]
    places = jnp.arange(known_rows.shape[0], dtype=jnp.int32)
    found_at = jnp.sum(jnp.where(matched, places[None, :], 0), axis=1)
    return (found_at, jnp.any(matched, axis=1))


def column_blocks(slot_values, row_ids, col_ids, owned_rows, column):
    selected = (row_ids[:, None] == owned_rows[None, :]) & (col_ids[:, None] == column)
    slot_places = jnp.arange(row_ids.shape[0], dtype=jnp.int32)
    slot_of = jnp.sum(jnp.where(selected, slot_places[:, None], 0), axis=0)
    present = jnp.any(selected, axis=0)
    return (jnp.where(present[:, None, None], slot_values[slot_of], 0.0), present)


def factor_and_send(raw_panel, owned_rows, coupled_rows, column):
    row_devices = lax.axis_size("row")
    col_devices = lax.axis_size("col")
    block_size = raw_panel.shape[-1]
    identity = jnp.eye(block_size, dtype=jnp.float32)
    at_pivot = owned_rows == column
    pivot_here = jnp.sum(jnp.where(at_pivot[:, None, None], raw_panel, 0.0), axis=0)
    pivot = broadcast(pivot_here, "row", column % row_devices)
    on_column = lax.axis_index("col") == column % col_devices
    pivot = jnp.where(on_column, pivot, identity)
    pivot_factor = jnp.linalg.cholesky(pivot)
    inverse = jax.scipy.linalg.solve_triangular(pivot_factor, identity, lower=True)
    scaled = jnp.einsum("mab,cb->mac", raw_panel, inverse, precision=exact_precision)
    local_panel = jnp.where(
        (owned_rows > column)[:, None, None],
        scaled,
        jnp.where(at_pivot[:, None, None], pivot_factor[None], 0.0),
    )
    row_panel = broadcast(local_panel, "col", column % col_devices)
    groups = row_devices // col_devices
    row_count = row_panel.shape[0]
    my_column = lax.axis_index("col")
    far_rows = lax.dynamic_index_in_dim(
        coupled_rows.reshape(groups, col_devices, row_count), my_column, 1, keepdims=False
    ).reshape(-1)
    received = []
    for group in range(groups):
        owner = my_column + group * col_devices
        received.append(broadcast(row_panel, "row", owner))
    far_panel = jnp.concatenate(received, axis=0)
    return (row_panel, far_panel, far_rows)


def apply_panel(slot_values, row_ids, col_ids, owned_rows, row_panel, far_panel, far_rows, column):
    row_slot, found_row = lookup(row_ids, owned_rows)
    col_slot, found_col = lookup(col_ids, far_rows)
    active = (col_ids > column) & found_col & found_row
    left_block = row_panel[row_slot]
    right_block = far_panel[col_slot]
    update_term = jnp.einsum("sab,scb->sac", left_block, right_block, precision=exact_precision)
    updated = slot_values - jnp.where(active[:, None, None], update_term, 0.0)
    in_column = (col_ids == column) & found_row
    return jnp.where(in_column[:, None, None], left_block, updated)


def body(values, block_ids, coupled_rows):
    slot_values = values[0, 0]
    row_ids = block_ids[0, 0, :, 0]
    col_ids = block_ids[0, 0, :, 1]
    owned_rows = lax.dynamic_index_in_dim(coupled_rows, lax.axis_index("row"), 0, keepdims=False)
    for column in range(PANELS):
        raw_panel, present = column_blocks(slot_values, row_ids, col_ids, owned_rows, column)
        row_panel, far_panel, far_rows = factor_and_send(
            raw_panel, owned_rows, coupled_rows, column
        )
        slot_values = apply_panel(
            slot_values, row_ids, col_ids, owned_rows, row_panel, far_panel, far_rows, column
        )
    slot_values = jnp.where((row_ids >= 0)[:, None, None], slot_values, 0.0)
    return slot_values[None, None]


def solution(mesh):
    placed = (P("row", "col", None, None, None), P("row", "col", None, None), P())
    return jax.shard_map(
        body,
        mesh=mesh,
        in_specs=placed,
        out_specs=P("row", "col", None, None, None),
        check_vma=False,
    )
```

profile of v0, /device:TPU:7, one launch (start us, length us, event | category | flops | bytes accessed | tf_op | source)
XLA Modules:
  0.0 752.4 jit_solution(18234598552750320994)
XLA Ops:
  13.8 50.3 %all-reduce.17.cloned.1.call-done = f32[128,128]{0,1:T(8,128)} async-done(((f32[128,128]{0,1:T(8,128)}), f32[128,128]{0,1:T(8,128)}) %all-reduce.17.cloned.1.call-update) | async-done | bytes 65552 | tf_op jit(solution)/shard_map/psum | solution.py:14
  65.9 11.7 %cholesky.74 = f32[128,128]{1,0:T(8,128)S(1)} custom-call(f32[128,128]{1,0:T(8,128)S(1)} %fusion.27), custom_call_target="Cholesky" | custom-call | tf_op jit(solution)/shard_map/jit(cholesky)/cholesky | solution.py:42
  79.0 9.8 %custom-call.8 = f32[1,128,128]{1,2,0:T(8,128)S(1)} custom-call(f32[1,128,128]{2,1,0:T(8,128)S(1)} %get-tuple-element.31), custom_call_target="InvertDiagBlocksLowerTriangular" | custom-call | tf_op jit(solution)/shard_map/jit(_solve_triangular)/triangular_solve | solution.py:43
  90.3 34.0 %all-reduce.19.cloned.1.call-done = f32[4,128,128]{2,1,0:T(8,128)} async-done(((f32[4,128,128]{2,1,0:T(8,128)}), f32[4,128,128]{2,1,0:T(8,128)}) %all-reduce.19.cloned.1.call-update) | async-done | bytes 262160 | tf_op jit(solution)/shard_map/psum | solution.py:14
  128.4 52.4 %all-reduce.39.cloned.1.call-done = (f32[4,128,128]{2,1,0:T(8,128)}, f32[4,128,128]{2,1,0:T(8,128)}) async-done(((f32[4,128,128]{2,1,0:T(8,128)}, f32[4,128,128]{2,1,0:T(8,128)}), (f32[4,128,128]{2,1,0:T(8,128)}, f32[4,128,128]{2,1,0:T(8,128)})) %all-reduce.39.cloned.1.call-update) | async-done | bytes 524304 | tf_op jit(solution)/shard_map/psum | solution.py:14
  184.0 8.8 %subtract_select_fusion.2 = f32[36,128,128]{2,1,0:T(8,128)S(1)} fusion(f32[36,128,128]{2,1,0:T(8,128)} %gather_fusion.1, f32[36,128,128]{2,1,0:T(8,128)} %gather_fusion.2, pred[36]{0:T(512)(128)(4,1)S(1)} %get-tuple-element.44, pred[36]{0:T(512)(128)(4,1)S(1)} %get-tuple-element.46, f32[1,1,36,128,128]{4,3,2,1,0:T(8,128)} %param.6), kind=kOutput, calls=%fused_computation.15 | convolution fusion | flops 907739136 | bytes 9437256 | tf_op jit(solution)/shard_map/sab,scb->sac/dot_general | solution.py:71
  194.5 51.8 %all-reduce.21.cloned.1.call-done = f32[128,128]{0,1:T(8,128)} async-done(((f32[128,128]{0,1:T(8,128)}), f32[128,128]{0,1:T(8,128)}) %all-reduce.21.cloned.1.call-update) | async-done | bytes 65552 | tf_op jit(solution)/shard_map/psum | solution.py:14
  246.5 11.7 %cholesky.85 = f32[128,128]{1,0:T(8,128)S(1)} custom-call(f32[128,128]{1,0:T(8,128)S(1)} %fusion.25), custom_call_target="Cholesky" | custom-call | tf_op jit(solution)/shard_map/jit(cholesky)/cholesky | solution.py:42
  259.5 9.8 %custom-call.9 = f32[1,128,128]{1,2,0:T(8,128)S(1)} custom-call(f32[1,128,128]{2,1,0:T(8,128)S(1)} %get-tuple-element.29), custom_call_target="InvertDiagBlocksLowerTriangular" | custom-call | tf_op jit(solution)/shard_map/jit(_solve_triangular)/triangular_solve | solution.py:43
  270.8 35.6 %all-reduce.23.cloned.1.call-done = f32[4,128,128]{2,1,0:T(8,128)} async-done(((f32[4,128,128]{2,1,0:T(8,128)}), f32[4,128,128]{2,1,0:T(8,128)}) %all-reduce.23.cloned.1.call-update) | async-done | bytes 262160 | tf_op jit(solution)/shard_map/psum | solution.py:14
  310.5 52.6 %all-reduce.37.cloned.1.call-done = (f32[4,128,128]{2,1,0:T(8,128)}, f32[4,128,128]{2,1,0:T(8,128)}) async-done(((f32[4,128,128]{2,1,0:T(8,128)}, f32[4,128,128]{2,1,0:T(8,128)}), (f32[4,128,128]{2,1,0:T(8,128)}, f32[4,128,128]{2,1,0:T(8,128)})) %all-reduce.37.cloned.1.call-update) | async-done | bytes 524304 | tf_op jit(solution)/shard_map/psum | solution.py:14
  366.3 8.7 %subtract_select_fusion.1 = f32[36,128,128]{2,1,0:T(8,128)S(1)} fusion(f32[36,128,128]{2,1,0:T(8,128)} %gather_fusion.4, f32[36,128,128]{2,1,0:T(8,128)} %copy-done.5, f32[36,128,128]{2,1,0:T(8,128)} %gather_fusion.5, pred[36]{0:T(512)(128)(4,1)S(1)} %get-tuple-element.43, pred[36]{0:T(512)(128)(4,1)S(1)} %get-tuple-element.48), kind=kOutput, calls=%fused_computation.14 | convolution fusion | flops 907739136 | bytes 9437256 | tf_op jit(solution)/shard_map/sab,scb->sac/dot_general | solution.py:71
  376.8 51.8 %all-reduce.25.cloned.1.call-done = f32[128,128]{0,1:T(8,128)} async-done(((f32[128,128]{0,1:T(8,128)}), f32[128,128]{0,1:T(8,128)}) %all-reduce.25.cloned.1.call-update) | async-done | bytes 65552 | tf_op jit(solution)/shard_map/psum | solution.py:14
  428.7 11.7 %cholesky.96 = f32[128,128]{1,0:T(8,128)S(1)} custom-call(f32[128,128]{1,0:T(8,128)S(1)} %fusion.23), custom_call_target="Cholesky" | custom-call | tf_op jit(solution)/shard_map/jit(cholesky)/cholesky | solution.py:42
  441.8 9.8 %custom-call.10 = f32[1,128,128]{1,2,0:T(8,128)S(1)} custom-call(f32[1,128,128]{2,1,0:T(8,128)S(1)} %get-tuple-element.27), custom_call_target="InvertDiagBlocksLowerTriangular" | custom-call | tf_op jit(solution)/shard_map/jit(_solve_triangular)/triangular_solve | solution.py:43
  453.1 36.4 %all-reduce.27.cloned.1.call-done = f32[4,128,128]{2,1,0:T(8,128)} async-done(((f32[4,128,128]{2,1,0:T(8,128)}), f32[4,128,128]{2,1,0:T(8,128)}) %all-reduce.27.cloned.1.call-update) | async-done | bytes 262160 | tf_op jit(solution)/shard_map/psum | solution.py:14
  493.6 52.5 %all-reduce.35.cloned.1.call-done = (f32[4,128,128]{2,1,0:T(8,128)}, f32[4,128,128]{2,1,0:T(8,128)}) async-done(((f32[4,128,128]{2,1,0:T(8,128)}, f32[4,128,128]{2,1,0:T(8,128)}), (f32[4,128,128]{2,1,0:T(8,128)}, f32[4,128,128]{2,1,0:T(8,128)})) %all-reduce.35.cloned.1.call-update) | async-done | bytes 524304 | tf_op jit(solution)/shard_map/psum | solution.py:14
  549.2 9.5 %subtract_select_fusion = f32[36,128,128]{2,1,0:T(8,128)} fusion(f32[36,128,128]{2,1,0:T(8,128)} %gather_fusion.7, f32[36,128,128]{2,1,0:T(8,128)S(1)} %subtract_select_fusion.1, f32[36,128,128]{2,1,0:T(8,128)} %gather_fusion.8, pred[36]{0:T(512)(128)(4,1)S(1)} %get-tuple-element.42, pred[36]{0:T(512)(128)(4,1)S(1)} %get-tuple-element.47), kind=kOutput, calls=%fused_computation.13 | convolution fusion | flops 907739136 | bytes 9437256 | tf_op jit(solution)/shard_map/sab,scb->sac/dot_general | solution.py:71
  562.1 51.7 %all-reduce.29.cloned.1.call-done = f32[128,128]{0,1:T(8,128)} async-done(((f32[128,128]{0,1:T(8,128)}), f32[128,128]{0,1:T(8,128)}) %all-reduce.29.cloned.1.call-update) | async-done | bytes 65552 | tf_op jit(solution)/shard_map/psum | solution.py:14
  614.0 11.7 %cholesky.107 = f32[128,128]{1,0:T(8,128)S(1)} custom-call(f32[128,128]{1,0:T(8,128)S(1)} %fusion.21), custom_call_target="Cholesky" | custom-call | tf_op jit(solution)/shard_map/jit(cholesky)/cholesky | solution.py:42
  627.1 9.8 %custom-call.11 = f32[1,128,128]{1,2,0:T(8,128)S(1)} custom-call(f32[1,128,128]{2,1,0:T(8,128)S(1)} %get-tuple-element.25), custom_call_target="InvertDiagBlocksLowerTriangular" | custom-call | tf_op jit(solution)/shard_map/jit(_solve_triangular)/triangular_solve | solution.py:43
  638.4 37.3 %all-reduce.31.cloned.1.call-done = f32[4,128,128]{2,1,0:T(8,128)} async-done(((f32[4,128,128]{2,1,0:T(8,128)}), f32[4,128,128]{2,1,0:T(8,128)}) %all-reduce.31.cloned.1.call-update) | async-done | bytes 262160 | tf_op jit(solution)/shard_map/psum | solution.py:14
  679.7 52.7 %all-reduce.33.cloned.1.call-done = (f32[4,128,128]{2,1,0:T(8,128)}, f32[4,128,128]{2,1,0:T(8,128)}) async-done(((f32[4,128,128]{2,1,0:T(8,128)}, f32[4,128,128]{2,1,0:T(8,128)}), (f32[4,128,128]{2,1,0:T(8,128)}, f32[4,128,128]{2,1,0:T(8,128)})) %all-reduce.33.cloned.1.call-update) | async-done | bytes 524304 | tf_op jit(solution)/shard_map/psum | solution.py:14
  735.6 9.5 %select_bitcast_fusion = f32[1,1,36,128,128]{4,3,2,1,0:T(8,128)} fusion(f32[36,128,128]{2,1,0:T(8,128)} %gather_fusion.10, f32[36,128,128]{2,1,0:T(8,128)S(1)} %copy-done.4, f32[36,128,128]{2,1,0:T(8,128)} %gather_fusion.11, pred[36]{0:T(512)(128)(4,1)S(1)} %get-tuple-element.41, pred[36]{0:T(512)(128)(4,1)S(1)} %get-tuple-element.45, ...), kind=kOutput, calls=%fused_computation.12 | convolution fusion | flops 908328960 | bytes 9437292 | tf_op jit(solution)/shard_map/sab,scb->sac/dot_general | solution.py:71
  (127 shorter events, 56.0 us)
Async XLA Ops:
  6.5 119.7 %copy-start.6 = (s32[1,1,36,2]{2,3,1,0:T(2,128)S(1)}, s32[1,1,36,2]{2,3,1,0:T(2,128)}, u32[]{:S(2)}) copy-start(s32[1,1,36,2]{2,3,1,0:T(2,128)} %param.7) | copy-start | bytes 868
  6.5 57.5 %all-reduce.17.cloned.1.call-start = ((), (), s32[]{:S(2)}) async-start(), calls=%async_computation | async-start | bytes 131072 | tf_op jit(solution)/shard_map/psum | solution.py:14
  12.5 111.8 %all-reduce.19.cloned.1.call-start = ((), (), s32[]{:S(2)}) async-start(), calls=%async_computation.1 | async-start | bytes 524288 | tf_op jit(solution)/shard_map/psum | solution.py:14
  90.2 90.6 %all-reduce.39.cloned.1.call-start = ((), (), s32[]{:S(2)}) async-start(), calls=%async_computation.11 | async-start | bytes 1048576 | tf_op jit(solution)/shard_map/psum | solution.py:14
  124.3 2.0 copy-start
  126.2 120.1 %all-reduce.21.cloned.1.call-start = ((), (), s32[]{:S(2)}) async-start(), calls=%async_computation.2 | async-start | bytes 131072 | tf_op jit(solution)/shard_map/psum | solution.py:14
  192.8 78.1 %copy-start.5 = (f32[36,128,128]{2,1,0:T(8,128)}, f32[36,128,128]{2,1,0:T(8,128)S(1)}, u32[]{:S(2)}) copy-start(f32[36,128,128]{2,1,0:T(8,128)S(1)} %subtract_select_fusion.2) | copy-start | bytes 7077892
  194.2 112.2 %all-reduce.23.cloned.1.call-start = ((), (), s32[]{:S(2)}) async-start(), calls=%async_computation.3 | async-start | bytes 524288 | tf_op jit(solution)/shard_map/psum | solution.py:14
  270.8 92.4 %all-reduce.37.cloned.1.call-start = ((), (), s32[]{:S(2)}) async-start(), calls=%async_computation.10 | async-start | bytes 1048576 | tf_op jit(solution)/shard_map/psum | solution.py:14
  306.5 1.9 copy-start.2
  308.3 120.2 %all-reduce.25.cloned.1.call-start = ((), (), s32[]{:S(2)}) async-start(), calls=%async_computation.4 | async-start | bytes 131072 | tf_op jit(solution)/shard_map/psum | solution.py:14
  376.5 113.0 %all-reduce.27.cloned.1.call-start = ((), (), s32[]{:S(2)}) async-start(), calls=%async_computation.5 | async-start | bytes 524288 | tf_op jit(solution)/shard_map/psum | solution.py:14
  453.0 93.0 %all-reduce.35.cloned.1.call-start = ((), (), s32[]{:S(2)}) async-start(), calls=%async_computation.9 | async-start | bytes 1048576 | tf_op jit(solution)/shard_map/psum | solution.py:14
  489.5 2.0 copy-start.1
  491.4 122.5 %all-reduce.29.cloned.1.call-start = ((), (), s32[]{:S(2)}) async-start(), calls=%async_computation.6 | async-start | bytes 131072 | tf_op jit(solution)/shard_map/psum | solution.py:14
  561.8 113.9 %all-reduce.31.cloned.1.call-start = ((), (), s32[]{:S(2)}) async-start(), calls=%async_computation.7 | async-start | bytes 524288 | tf_op jit(solution)/shard_map/psum | solution.py:14
  638.3 94.1 %all-reduce.33.cloned.1.call-start = ((), (), s32[]{:S(2)}) async-start(), calls=%async_computation.8 | async-start | bytes 1048576 | tf_op jit(solution)/shard_map/psum | solution.py:14
  675.7 1.9 copy-start.3
  733.5 2.2 copy-start.4
Sparse Core Ops, SparseCore 0:
  12.6 51.4 all-reduce.16
  90.3 33.9 all-reduce.18
  127.4 53.3 all-reduce.38
  194.4 51.9 all-reduce.20
  270.9 35.5 all-reduce.22
  309.8 53.3 all-reduce.36
  376.6 51.8 all-reduce.24
  453.2 36.2 all-reduce.26
  492.6 53.3 all-reduce.34
  561.9 51.8 all-reduce.28
  638.5 37.2 all-reduce.30
  679.0 53.3 all-reduce.32
where the time goes:
time: 765 us; the launch traced here: 752 us
  waiting for transfers between devices  559 us (73%)
  other arithmetic  109 us (14%)
  matrix products  42.2 us (6%)
  local copies, waits for them, and re-layouts  25.8 us (3%)
  between operations  14.5 us (2%)
    psum x12, waiting for transfers between devices, broadcast(): return lax.psum(jnp.where(mine, shard, jnp.zeros_like(shard)), axis)  559 us
    another operation x12, other arithmetic, factor_and_send(): pivot_factor = jnp.linalg.cholesky(pivot)  49.6 us
    another operation x8, other arithmetic, factor_and_send(): jax.scipy.linalg.solve_triangular(pivot_factor, identity, lower=True)  41.9 us
    dot_general x4, matrix products, apply_panel(): jnp.einsum('sab,scb->sac', left_block, right_block, precision=exact_preci...  36.5 us
  transfers between devices with their start and end apart: 12, of which 12 were waited for; matrix products, arithmetic and copies ran while one was open for 1% of the time, Pallas kernels for 0%

commit v1 on v0

v1 whole, which is shorter than its diff:
```python
import functools

import jax
import jax.numpy as jnp
from jax import lax
from jax.experimental import pallas as pl
from jax.experimental.pallas import tpu as pltpu
from jax.sharding import PartitionSpec as P

PANELS = 4
GROUP = 32
SUB = 8
STRIPS = GROUP // SUB
F32 = jnp.float32
BF16 = jnp.bfloat16
HIGHEST = lax.Precision.HIGHEST
HBM = pl.BlockSpec(memory_space=pl.ANY)
SMEM = pl.BlockSpec(memory_space=pltpu.SMEM)
VMEM = pl.BlockSpec(memory_space=pltpu.VMEM)


def find(ids, rows, place, slots):
    me, column = lax.axis_index("row"), lax.axis_index("col")
    places = lax.broadcasted_iota(jnp.int32, (1, slots), 1)
    hit = (ids[1:2, :] == column) & (ids[0:1, :] == rows[place, me])
    return jnp.max(jnp.where(hit, places, -1))


def extract_kernel(col_devices, ids, rows, values, head, tail, table, sems):
    slots, count = values.shape[0], rows.shape[0]
    groups = rows.shape[1] // col_devices
    me = lax.axis_index("row")
    column = lax.axis_index("col")
    copies, present = [], []
    for place in range(count):
        found = find(ids, rows, place, slots)
        present.append(found >= 0)
        target = head.at[0] if place == 0 else tail.at[place - 1]
        copy = pltpu.make_async_copy(values.at[jnp.maximum(found, 0)], target, sems.at[place])
        copy.start()
        copies.append(copy)
    row_ids, col_ids = ids[0:1, :], ids[1:2, :]
    row_place = jnp.full((1, slots), -1, jnp.int32)
    col_place = jnp.full((1, slots), -1, jnp.int32)
    for place in range(count):
        row_place = jnp.where(row_ids == rows[place, me], place, row_place)
        for group in range(groups):
            known = rows[place, column + group * col_devices]
            col_place = jnp.where(col_ids == known, group * count + place, col_place)
    both = (row_place >= 0) & (col_place >= 0)
    kind = jnp.where(row_ids < 0, 0, jnp.where(both, jnp.where(col_ids < PANELS, 2, 3), 1))
    table[0:1, :] = kind
    table[1:2, :] = jnp.maximum(row_place, 0)
    table[2:3, :] = jnp.maximum(col_place, 0)
    for place, copy in enumerate(copies):
        copy.wait()
        if place == 0:
            head[0] = jnp.where(present[place], head[0], 0.0)
        else:
            tail[place - 1] = jnp.where(present[place], tail[place - 1], 0.0)


def extract(ids, rows, values, col_devices):
    slots, size, _ = values.shape
    count = rows.shape[0]
    return pl.pallas_call(
        functools.partial(extract_kernel, col_devices),
        name="extract",
        in_specs=[VMEM, SMEM, HBM],
        out_specs=[VMEM, VMEM, VMEM],
        out_shape=[
            jax.ShapeDtypeStruct((1, size, size), F32),
            jax.ShapeDtypeStruct((count - 1, size, size), F32),
            jax.ShapeDtypeStruct((3, slots), jnp.int32),
        ],
        scratch_shapes=[pltpu.SemaphoreType.DMA((count,))],
    )(ids, rows, values)


def one_row(strip, place):
    return jnp.broadcast_to(strip[place : place + 1, :], strip.shape)


def eliminate(upper, extra, diagonal):
    width = upper[0].shape[1]
    sublane = lax.broadcasted_iota(jnp.int32, (SUB, width), 0)
    cols = [
        [
            jnp.broadcast_to(diagonal[q][:, t : t + 1], (SUB, width)) if q >= t // SUB else None
            for q in range(STRIPS)
        ]
        for t in range(GROUP)
    ]
    scale = [jnp.zeros((SUB, width), F32)] * STRIPS
    for t in range(GROUP):
        strip, place = divmod(t, SUB)
        pivot = one_row(cols[t][strip], place)
        reciprocal = 1.0 / pivot
        scale[strip] = jnp.where(sublane == place, lax.rsqrt(pivot), scale[strip])
        factor = {q: cols[t][q] * reciprocal for q in range(strip, STRIPS)}
        factor[strip] = jnp.where(sublane > place, factor[strip], 0.0)
        for u in range(t + 1, GROUP):
            entry = one_row(cols[t][u // SUB], u % SUB)
            for q in range(u // SUB, STRIPS):
                cols[u][q] = cols[u][q] - factor[q] * entry
        pivot_upper = one_row(upper[strip], place)
        pivot_extra = one_row(extra[strip], place)
        for q in range(strip, STRIPS):
            upper[q] = upper[q] - factor[q] * pivot_upper
            extra[q] = extra[q] - factor[q] * pivot_extra
    upper = jnp.concatenate([upper[q] * scale[q] for q in range(STRIPS)], axis=0)
    extra = jnp.concatenate([extra[q] * scale[q] for q in range(STRIPS)], axis=0)
    return upper, extra


def exact(a, b):
    return jnp.dot(a, b, precision=HIGHEST, preferred_element_type=F32)


def exact_t(a, b):
    return lax.dot_general(
        a, b, (((1,), (1,)), ((), ())), precision=HIGHEST, preferred_element_type=F32
    )


def factor_block(block, work, extra_work):
    size = block.shape[0]
    row_place = lax.broadcasted_iota(jnp.int32, (size, size), 0)
    col_place = lax.broadcasted_iota(jnp.int32, (size, size), 1)
    work[...] = block
    extra_work[...] = jnp.where(row_place == col_place, 1.0, 0.0)
    uppers, extras = [], []
    for start in range(0, size, GROUP):
        strips = [pl.ds(start + q * SUB, SUB) for q in range(STRIPS)]
        upper = [work[s, :] for s in strips]
        extra = [extra_work[s, :] for s in strips]
        diagonal = [strip[:, start : start + GROUP] for strip in upper]
        upper, extra = eliminate(upper, extra, diagonal)
        uppers.append(upper)
        extras.append(extra)
        end = start + GROUP
        if end < size:
            left = upper[:, end:].T
            work[end:, :] = work[end:, :] - exact(left, upper)
            extra_work[end:, :] = extra_work[end:, :] - exact(left, extra)
    upper = jnp.concatenate(uppers, axis=0)
    inverse = jnp.where(row_place >= col_place, jnp.concatenate(extras, axis=0), 0.0)
    return jnp.where(row_place <= col_place, upper, 0.0), inverse


def halves(x):
    high = x.astype(BF16)
    return high, (x - high.astype(F32)).astype(BF16)


def lead_kernel(near, across, factor, inv_hi, inv_lo, lead, inverse, work, extra_work):
    size = near.shape[-1]
    me = lax.axis_index("row")
    column = lax.axis_index("col")
    for row in range(PANELS):
        for col in range(row + 1):
            flip_x = ((me // 2) % 2) ^ (row // 2)
            flip_core = (me % 2) ^ (row % 2)
            place = column ^ col

            @pl.when(flip_core == 0)
            def _():
                lead[row, col] = near[flip_x, place]

            @pl.when(flip_core == 1)
            def _():
                lead[row, col] = across[flip_x, place]

    zero = jnp.zeros((size, size), F32)
    for k in range(PANELS):
        upper, inv = factor_block(lead[k, k], work, extra_work)
        lead[k, k] = upper.T
        for i in range(k + 1, PANELS):
            lead[i, k] = exact_t(lead[i, k], inv)
        for i in range(k + 1, PANELS):
            for j in range(k + 1, i + 1):
                lead[i, j] = lead[i, j] - exact_t(lead[i, k], lead[j, k])
        for j in range(PANELS):
            rows, cols = slice(k * size, (k + 1) * size), slice(j * size, (j + 1) * size)
            if j > k:
                inverse[rows, cols] = zero
            elif j == k:
                inverse[rows, cols] = inv
            else:
                total = zero
                for m in range(j, k):
                    total = total + exact(
                        lead[k, m], inverse[m * size : (m + 1) * size, j * size : (j + 1) * size]
                    )
                inverse[rows, cols] = -exact(inv, total)
    inv_hi[...], inv_lo[...] = halves(inverse[...])
    factor[...] = lead[jnp.minimum(me, PANELS - 1), jnp.minimum(column, PANELS - 1)]


def factor_lead(near, across):
    size = near.shape[-1]
    width = PANELS * size
    return pl.pallas_call(
        lead_kernel,
        name="factor_lead",
        in_specs=[VMEM, VMEM],
        out_specs=[VMEM, VMEM, VMEM],
        out_shape=[
            jax.ShapeDtypeStruct((size, size), F32),
            jax.ShapeDtypeStruct((width, width), BF16),
            jax.ShapeDtypeStruct((width, width), BF16),
        ],
        scratch_shapes=[
            pltpu.VMEM((PANELS, PANELS, size, size), F32),
            pltpu.VMEM((width, width), F32),
            pltpu.VMEM((size, size), F32),
            pltpu.VMEM((size, size), F32),
        ],
        compiler_params=pltpu.CompilerParams(vmem_limit_bytes=16 * 2**20),
        cost_estimate=pl.CostEstimate(flops=2**34, bytes_accessed=2**25, transcendentals=0),
    )(near, across)


def dot3_t(a, b):
    dims = (((1,), (1,)), ((), ()))
    dot = functools.partial(lax.dot_general, dimension_numbers=dims, preferred_element_type=F32)
    return dot(a[0], b[0]) + (dot(a[0], b[1]) + dot(a[1], b[0]))


def update_kernel(plan, table, *refs):
    groups, count, col_devices = plan
    refs = list(refs)
    heads = [refs.pop(0) for _ in range(col_devices)]
    tails = [refs.pop(0) for _ in range(col_devices)]
    others = [None, None] + [refs.pop(0) for _ in range(2, col_devices)]
    near = [refs.pop(0) for _ in range(groups)]
    across = [refs.pop(0) for _ in range(groups)]
    factor, inv_hi, inv_lo, values, out = [refs.pop(0) for _ in range(5)]
    raw, high, low, product, slots_in, sems, io_sems = refs
    slots, size, _ = values.shape
    own_rows = count * size
    far_rows = groups * own_rows
    me = lax.axis_index("row")
    column = lax.axis_index("col")

    load = pltpu.make_async_copy(values, slots_in, io_sems.at[0])
    load.start()
    same_core = ((me ^ column) % 2) == 0
    owner = ((me ^ column) % col_devices) == 0
    for p in range(col_devices):
        col = column ^ p

        @pl.when(col < PANELS)
        def _():
            lanes = pl.ds(pl.multiple_of(jnp.minimum(col, PANELS - 1) * size, size), size)
            for place in range(count):
                target = raw.at[pl.ds(place * size, size), lanes]
                if place == 0 or p < 2:
                    source = heads[p].at[0] if place == 0 else tails[p].at[place - 1]
                    pltpu.make_async_copy(source, target, sems.at[0]).start()
                    continue

                @pl.when(owner)
                def _():
                    pltpu.make_async_copy(tails[p].at[place - 1], target, sems.at[0]).start()

                @pl.when(jnp.logical_not(owner))
                def _():
                    pltpu.make_async_copy(others[p].at[place - 1], target, sems.at[0]).start()

            for q in range(groups):
                group = (me // col_devices) ^ q
                for place in range(count):
                    block = p * count + place
                    rows = pl.ds(
                        pl.multiple_of(own_rows + (group * count + place) * size, size), size
                    )

                    @pl.when(same_core)
                    def _():
                        pltpu.make_async_copy(
                            near[q].at[block], raw.at[rows, lanes], sems.at[1]
                        ).start()

                    @pl.when(jnp.logical_not(same_core))
                    def _():
                        pltpu.make_async_copy(
                            across[q].at[block], raw.at[rows, lanes], sems.at[1]
                        ).start()

    half = PANELS * size // 2
    for part in range(groups + 1):
        if part < 2:
            arrived = raw.at[:own_rows, :] if part == 0 else raw.at[own_rows:, :]
            pltpu.make_async_copy(arrived, arrived, sems.at[part]).wait()
        rows = pl.ds(part * own_rows, own_rows)
        hi, lo = halves(raw[rows, :])
        first = dot3_t(
            (hi[:, :half], lo[:, :half]), (inv_hi[:half, :half], inv_lo[:half, :half])
        )
        second = dot3_t((hi, lo), (inv_hi[half:, :], inv_lo[half:, :]))
        if part == 0:
            raw[rows, :half], raw[rows, half:] = first, second
        high[rows, :half], low[rows, :half] = halves(first)
        high[rows, half:], low[rows, half:] = halves(second)
    load.wait()
    own = pl.ds(0, own_rows)
    for start in range(0, far_rows, 2 * size):
        rows = pl.ds(own_rows + start, 2 * size)
        result = dot3_t((high[own, :], low[own, :]), (high[rows, :], low[rows, :]))
        for place in range(count):
            for side in range(2):
                product[place, start // size + side] = result[
                    place * size : (place + 1) * size, side * size : (side + 1) * size
                ]
    lead_row = me < PANELS
    lead_col = jnp.minimum(column, PANELS - 1)
    lanes = pl.ds(pl.multiple_of(lead_col * size, size), size)

    def finish(slot, carry):
        kind, row, col = table[0, slot], table[1, slot], table[2, slot]

        @pl.when(kind == 0)
        def _():
            slots_in[slot] = jnp.zeros((size, size), F32)

        @pl.when(kind == 3)
        def _():
            slots_in[slot] = slots_in[slot] - product[row, col]

        @pl.when((kind == 2) & lead_row & (row == 0))
        def _():
            slots_in[slot] = factor[...]

        @pl.when((kind == 2) & jnp.logical_not(lead_row & (row == 0)))
        def _():
            slots_in[slot] = raw[pl.ds(pl.multiple_of(row * size, size), size), lanes]

        pltpu.make_async_copy(slots_in.at[slot], out.at[slot], io_sems.at[1]).start()
        return carry

    lax.fori_loop(0, slots, finish, 0)
    pltpu.make_async_copy(slots_in, out, io_sems.at[1]).wait()


def update(table, heads, tails, others, near, across, solved_lead, values, col_devices):
    slots, size, _ = values.shape
    groups, count = len(near), tails[0].shape[0] + 1
    flat = [*heads, *tails, *others, *near, *across]
    width = PANELS * size
    rows = (groups + 1) * count * size
    return pl.pallas_call(
        functools.partial(update_kernel, (groups, count, col_devices)),
        name="update",
        in_specs=[SMEM] + [HBM] * len(flat) + [VMEM, VMEM, VMEM, HBM],
        out_specs=HBM,
        out_shape=jax.ShapeDtypeStruct(values.shape, F32),
        scratch_shapes=[
            pltpu.VMEM((rows, width), F32),
            pltpu.VMEM((rows, width), BF16),
            pltpu.VMEM((rows, width), BF16),
            pltpu.VMEM((count, groups * count, size, size), F32),
            pltpu.VMEM((slots, size, size), F32),
            pltpu.SemaphoreType.DMA((2,)),
            pltpu.SemaphoreType.DMA((2,)),
        ],
        compiler_params=pltpu.CompilerParams(vmem_limit_bytes=24 * 2**20),
    )(table, *flat, *solved_lead, values)


def pack_kernel(pieces, *refs):
    heads, tails = refs[:pieces], refs[pieces : 2 * pieces]
    packed, sem = refs[-2:]
    count = packed.shape[0] // pieces
    for p in range(pieces):
        at = p * count
        pltpu.make_async_copy(heads[p], packed.at[at : at + 1], sem).start()
        pltpu.make_async_copy(tails[p], packed.at[at + 1 : at + count], sem).start()
    pltpu.make_async_copy(packed, packed, sem).wait()


def pack(heads, tails):
    size = heads[0].shape[-1]
    blocks = sum(x.shape[0] for x in (*heads, *tails))
    operands = [*heads, *tails]
    return pl.pallas_call(
        functools.partial(pack_kernel, len(heads)),
        name="pack",
        in_specs=[HBM] * len(operands),
        out_specs=VMEM,
        out_shape=jax.ShapeDtypeStruct((blocks, size, size), F32),
        scratch_shapes=[pltpu.SemaphoreType.DMA],
    )(*operands)


def body(values, block_ids, coupled_rows):
    row_devices, col_devices = lax.axis_size("row"), lax.axis_size("col")
    every_row, every_col = range(row_devices), range(col_devices)
    groups = row_devices // col_devices
    me, column = lax.axis_index("row"), lax.axis_index("col")
    slot_values = values[0, 0]
    rows = coupled_rows.T

    def send(x, flip, keep=lambda r, c: True):
        pairs = [
            (r * col_devices + c, (r ^ flip) * col_devices + c)
            for r in every_row
            for c in every_col
            if keep(r, c)
        ]
        return lax.ppermute(x, ("row", "col"), pairs)

    def over_col(x, flips, keep=lambda r, c: True):
        got = []
        for p in flips:
            pairs = [
                (r * col_devices + c, r * col_devices + (c ^ p))
                for r in every_row
                for c in range(PANELS)
                if keep(r, c ^ p)
            ]
            got.append(lax.ppermute(x, ("row", "col"), pairs))
        return got

    def owner(r, c):
        return (r ^ c) % col_devices == 0

    head, tail, table = extract(block_ids[0, 0].T, rows, slot_values, col_devices)
    heads = [head, *over_col(head, range(1, col_devices))]
    tails = [tail, *over_col(tail, [1]), *over_col(tail, range(2, col_devices), owner)]

    mine = jnp.concatenate(heads, axis=0)
    flips = [high + low for high in range(0, row_devices, PANELS) for low in (0, 2)]
    arrived = [mine if flip == 0 else send(mine, flip, lambda r, c: r < PANELS) for flip in flips]
    arrived, tails = lax.optimization_barrier((arrived, tails))
    same, beside = arrived[:2]
    for flip, got, got_beside in zip(flips[2::2], arrived[2::2], arrived[3::2]):
        here = (me // PANELS) * PANELS == flip
        same, beside = jnp.where(here, got, same), jnp.where(here, got_beside, beside)
    near_lead = jnp.stack([same, beside])
    across_lead = send(near_lead, 1)
    solved_lead = factor_lead(near_lead, across_lead)

    owned = pack(heads, tails)
    others = over_col(tail, range(2, col_devices), lambda r, c: not owner(r, c))
    flips = [q * col_devices + low for q in range(groups) for low in range(0, col_devices, 2)]
    far = [owned if flip == 0 else send(owned, flip, owner) for flip in flips]
    far, others, solved_lead = lax.optimization_barrier((far, others, solved_lead))
    near, across = [], []
    for q in range(groups):
        part = None
        for flip, got in zip(flips, far):
            if flip // col_devices == q:
                here = (me ^ column) % col_devices // 2 * 2 == flip % col_devices
                part = got if part is None else jnp.where(here, got, part)
        near.append(part)
        across.append(send(part, 1, lambda r, c: (r ^ c) % 2 == 0))

    result = update(
        table, heads, tails, others, near, across, solved_lead, slot_values, col_devices
    )
    return result[None, None]


def solution(mesh):
    placed = (P("row", "col", None, None, None), P("row", "col", None, None), P())
    return jax.shard_map(
        body,
        mesh=mesh,
        in_specs=placed,
        out_specs=P("row", "col", None, None, None),
        check_vma=False,
    )
```

time: 765 us -> 79.8 us (0.10); the launches traced: 752 us -> 79.3 us
  waiting for transfers between devices: 559 us -> 22.6 us
  other arithmetic: 109 us -> 0.31 us
  matrix products: 42.2 us -> 0 us
  Pallas kernels: 0 us -> 29.5 us
  local copies, waits for them, and re-layouts: 25.8 us -> 0.95 us
  starting transfers between devices: 1.1 us -> 25.3 us
  between operations: 14.5 us -> 0.69 us
    psum x12 -> x0, waiting for transfers between devices: 559 us -> none  [broadcast(): return lax.psum(jnp.where(mine, shard, jnp.zeros_like(shard)), axis)]
    another operation x20 -> x2, other arithmetic: 91.4 us -> 0.09 us  [body(): near_lead = jnp.stack([same, beside])]
    dot_general x8 -> x0, matrix products: 41 us -> none  [the longest x4 36.5 us: apply_panel(): jnp.einsum('sab,scb->sac', left_block, right_block, precision=exact_preci...]
    pallas_call x0 -> x4, Pallas kernels: none -> 29.5 us  [the longest x1 17 us: factor_lead(): pl.pallas_call(lead_kernel, name='factor_lead', in_specs=[VMEM, VMEM], ou...]
    ppermute x0 -> x17, starting transfers between devices: none -> 25.3 us  [the longest x8 16.5 us: over_col(): got.append(lax.ppermute(x, ('row', 'col'), pairs))]
    ppermute x0 -> x17, waiting for transfers between devices: none -> 22.6 us  [the longest x9 18.4 us: send(): return lax.ppermute(x, ('row', 'col'), pairs)]
    gather x12 -> x0, local copies, waits for them, and re-layouts: 22.4 us -> none  [the longest x4 8.44 us: apply_panel(): right_block = far_panel[col_slot]]
    select_n x18 -> x2, other arithmetic: 10.9 us -> 0.22 us  [body(): part = got if part is None else jnp.where(here, got, part)]
  transfers between devices with their start and end apart: 12 -> 17, of which waited for: 12 -> 4; matrix products, arithmetic and copies ran while one was open for 1% -> 1% of each run, Pallas kernels for 0% -> 24%
where the time goes in v1:
time: 79.8 us; the launch traced here: 79.3 us
  Pallas kernels  29.5 us (37%)
  starting transfers between devices  25.3 us (32%)
  waiting for transfers between devices  22.6 us (28%)
  local copies, waits for them, and re-layouts  0.95 us (1%)
    ppermute x9, waiting for transfers between devices, send(): return lax.ppermute(x, ('row', 'col'), pairs)  18.4 us
    pallas_call x1, Pallas kernels, factor_lead(): pl.pallas_call(lead_kernel, name='factor_lead', in_specs=[VMEM, VMEM], ou...  17 us
    ppermute x8, starting transfers between devices, over_col(): got.append(lax.ppermute(x, ('row', 'col'), pairs))  16.5 us
    ppermute x9, starting transfers between devices, send(): return lax.ppermute(x, ('row', 'col'), pairs)  8.85 us
    pallas_call x1, Pallas kernels, update(): pl.pallas_call(functools.partial(update_kernel, (groups, count, col_devic...  7.45 us
    ppermute x8, waiting for transfers between devices, over_col(): got.append(lax.ppermute(x, ('row', 'col'), pairs))  4.16 us
    pallas_call x1, Pallas kernels, extract(): pl.pallas_call(functools.partial(extract_kernel, col_devices), name='extr...  2.71 us
    pallas_call x1, Pallas kernels, pack(): pl.pallas_call(functools.partial(pack_kernel, len(heads)), name='pack', i...  2.26 us
  transfers between devices with their start and end apart: 17, of which 4 were waited for; matrix products, arithmetic and copies ran while one was open for 1% of the time, Pallas kernels for 24%

profile of v1, /device:TPU:7, one launch (start us, length us, event | category | flops | bytes accessed | tf_op | source)
XLA Modules:
  0.0 79.3 jit_solution(18063248627202877435)
XLA Ops:
  0.0 2.7 %extract.1 = (f32[1,128,128]{2,1,0:T(8,128)}, f32[3,128,128]{2,1,0:T(8,128)}, s32[3,36]{1,0:T(4,128)}) custom-call(s32[2,36]{1,0:T(2,128)} %bitcast.13, s32[4,8]{1,0:T(4,128)} %bitcast.12, f32[36,128,128]{2,1,0:T(8,128)} %bitcast.10), custom_call_target="tpu_custom_call" | custom-call | tf_op jit(solution)/shard_map/extract/pallas_call | solution.py:66
  2.7 3.4 %collective-permute-start.2 = (f32[1,128,128]{2,1,0:T(8,128)}, f32[1,128,128]{2,1,0:T(8,128)S(1)}, u32[]{:S(2)}, u32[]{:S(2)}) collective-permute-start(f32[1,128,128]{2,1,0:T(8,128)} %get-tuple-element.29.refs_0_), channel_id=1, source_target_pairs={{0,3},{1,2},{2,1},{3,0},{4,7},{5,6},{6,5},{7,4},{8,11},{9,10},{10,... | collective-permute-start | bytes 196616 | tf_op jit(solution)/shard_map/ppermute | solution.py:422
  6.5 5.1 %collective-permute-start.8 = (f32[3,128,128]{2,1,0:T(8,128)}, f32[3,128,128]{2,1,0:T(8,128)S(1)}, u32[]{:S(2)}, u32[]{:S(2)}) collective-permute-start(f32[3,128,128]{2,1,0:T(8,128)} %get-tuple-element.31.refs_4_), channel_id=1, source_target_pairs={{3,0},{6,5},{9,10},{12,15},{19,16},{22,21},{25,26},{28,31}} | collective-permute-start | bytes 589832 | tf_op jit(solution)/shard_map/ppermute | solution.py:422
  11.6 0.8 %constant_dynamic-update-slice_fusion.3 = f32[4,128,128]{2,1,0:T(8,128)S(1)} fusion(f32[1,128,128]{2,1,0:T(8,128)} %get-tuple-element.29.refs_0_), kind=kLoop, calls=%fused_computation.8 | loop fusion | bytes 131072
  12.5 1.3 %collective-permute-start.5 = (f32[4,128,128]{2,1,0:T(8,128)S(1)}, f32[4,128,128]{2,1,0:T(8,128)S(1)}, u32[]{:S(2)}, u32[]{:S(2)}) collective-permute-start(f32[4,128,128]{2,1,0:T(8,128)S(1)} %constant_dynamic-update-slice_fusion), channel_id=1, source_target_pairs={{0,24},{1,25},{2,26},{3,27},{4,28},{5,29},{6,30},{7,31},{8,16},{9,... | collective-permute-start | bytes 786440 | tf_op jit(solution)/shard_map/ppermute | solution.py:411
  13.8 1.3 %collective-permute-start.4 = (f32[4,128,128]{2,1,0:T(8,128)S(1)}, f32[4,128,128]{2,1,0:T(8,128)S(1)}, u32[]{:S(2)}, u32[]{:S(2)}) collective-permute-start(f32[4,128,128]{2,1,0:T(8,128)S(1)} %constant_dynamic-update-slice_fusion), channel_id=1, source_target_pairs={{0,16},{1,17},{2,18},{3,19},{4,20},{5,21},{6,22},{7,23},{8,24},{9,... | collective-permute-start | bytes 786440 | tf_op jit(solution)/shard_map/ppermute | solution.py:411
  15.1 0.7 collective-permute-start.3
  15.8 0.7 collective-permute-start.7
  16.5 2.5 %collective-permute-start.6 = (f32[3,128,128]{2,1,0:T(8,128)}, f32[3,128,128]{2,1,0:T(8,128)S(1)}, u32[]{:S(2)}, u32[]{:S(2)}) collective-permute-start(f32[3,128,128]{2,1,0:T(8,128)} %get-tuple-element.31.refs_4_), channel_id=1, source_target_pairs={{0,1},{1,0},{2,3},{3,2},{4,5},{5,4},{6,7},{7,6},{8,9},{9,8},{10,11... | collective-permute-start | bytes 589832 | tf_op jit(solution)/shard_map/ppermute | solution.py:422
  19.0 4.1 %collective-permute-done.6.refs_5_ = f32[3,128,128]{2,1,0:T(8,128)S(1)} collective-permute-done((f32[3,128,128]{2,1,0:T(8,128)}, f32[3,128,128]{2,1,0:T(8,128)S(1)}, u32[]{:S(2)}, u32[]{:S(2)}) %collective-permute-start.6) | collective-permute-done | bytes 196640 | tf_op jit(solution)/shard_map/ppermute | solution.py:422
  23.2 6.0 %collective-permute-done.4 = f32[4,128,128]{2,1,0:T(8,128)S(1)} collective-permute-done((f32[4,128,128]{2,1,0:T(8,128)S(1)}, f32[4,128,128]{2,1,0:T(8,128)S(1)}, u32[]{:S(2)}, u32[]{:S(2)}) %collective-permute-start.4) | collective-permute-done | bytes 262176 | tf_op jit(solution)/shard_map/ppermute | solution.py:411
  29.3 0.6 collective-permute-start.14
  29.8 1.3 %collective-permute-start.13 = (f32[3,128,128]{2,1,0:T(8,128)S(1)}, f32[3,128,128]{2,1,0:T(8,128)S(1)}, u32[]{:S(2)}, u32[]{:S(2)}) collective-permute-start(f32[3,128,128]{2,1,0:T(8,128)S(1)} %copy-done.1), channel_id=1, source_target_pairs={{0,3},{1,2},{2,1},{4,7},{5,6},{7,4},{8,11},{10,9},{11,8},{13,14},{... | collective-permute-start | bytes 589832 | tf_op jit(solution)/shard_map/ppermute | solution.py:422
  31.1 3.2 %collective-permute-start.12 = (f32[3,128,128]{2,1,0:T(8,128)S(1)}, f32[3,128,128]{2,1,0:T(8,128)S(1)}, u32[]{:S(2)}, u32[]{:S(2)}) collective-permute-start(f32[3,128,128]{2,1,0:T(8,128)S(1)} %copy-done.1), channel_id=1, source_target_pairs={{0,2},{1,3},{3,1},{4,6},{5,7},{6,4},{9,11},{10,8},{11,9},{12,14},{... | collective-permute-start | bytes 589832 | tf_op jit(solution)/shard_map/ppermute | solution.py:422
  34.4 2.3 %pack.1 = f32[16,128,128]{2,1,0:T(8,128)} custom-call(f32[1,128,128]{2,1,0:T(8,128)} %get-tuple-element.29.refs_0_, f32[1,128,128]{2,1,0:T(8,128)} %copy-done.14, f32[1,128,128]{2,1,0:T(8,128)} %copy-done.12, f32[1,128,128]{2,1,0:T(8,128)} %copy-done.10, f32[3,128,128]{2,1,0:T(8,128)} %get-tuple-element.31.refs_4_, f32[3,128,128]{2,1,0:T(8,128)} %copy-done.7, ...), custom_call_target="tpu_custom_call" | custom-call | tf_op jit(solution)/shard_map/pack/pallas_call | solution.py:386
  36.7 0.7 collective-permute-start.11
  37.4 0.7 collective-permute-start.10
  38.1 0.7 collective-permute-start.9
  38.9 17.0 %factor_lead.1 = (f32[128,128]{1,0:T(8,128)S(1)}, bf16[512,512]{1,0:T(8,128)(2,1)S(1)}, bf16[512,512]{1,0:T(8,128)(2,1)S(1)}) custom-call(f32[2,4,128,128]{3,2,1,0:T(8,128)S(1)} %pad_maximum_fusion.near, f32[2,4,128,128]{3,2,1,0:T(8,128)S(1)} %collective-permute-done.14.across), custom_call_target="tpu_custom_call" | custom-call | flops 17179869184 | bytes 33554432 | tf_op jit(solution)/shard_map/factor_lead/pallas_call | solution.py:203
  56.2 1.6 %collective-permute-start.16 = (f32[16,128,128]{2,1,0:T(8,128)S(1)}, f32[16,128,128]{2,1,0:T(8,128)S(1)}, u32[]{:S(2)}, u32[]{:S(2)}) collective-permute-start(f32[16,128,128]{2,1,0:T(8,128)S(1)} %broadcast_select_fusion.refs_11_), channel_id=1, source_target_pairs={{0,4},{2,6},{5,1},{7,3},{8,12},{10,14},{13,9},{15,11},{16,20},{18,... | collective-permute-start | bytes 3145736 | tf_op jit(solution)/shard_map/ppermute | solution.py:411
  57.9 1.3 %collective-permute-start.15 = (f32[16,128,128]{2,1,0:T(8,128)S(1)}, f32[16,128,128]{2,1,0:T(8,128)S(1)}, u32[]{:S(2)}, u32[]{:S(2)}) collective-permute-start(f32[16,128,128]{2,1,0:T(8,128)S(1)} %broadcast_select_fusion.1.refs_10_), channel_id=1, source_target_pairs={{0,4},{2,6},{5,1},{7,3},{8,12},{10,14},{13,9},{15,11},{16,20},{18,... | collective-permute-start | bytes 3145736 | tf_op jit(solution)/shard_map/ppermute | solution.py:411
  59.2 10.9 %collective-permute-done.16.refs_13_ = f32[16,128,128]{2,1,0:T(8,128)S(1)} collective-permute-done((f32[16,128,128]{2,1,0:T(8,128)S(1)}, f32[16,128,128]{2,1,0:T(8,128)S(1)}, u32[]{:S(2)}, u32[]{:S(2)}) %collective-permute-start.16) | collective-permute-done | bytes 1048608 | tf_op jit(solution)/shard_map/ppermute | solution.py:411
  70.1 1.5 %collective-permute-done.15.refs_12_ = f32[16,128,128]{2,1,0:T(8,128)S(1)} collective-permute-done((f32[16,128,128]{2,1,0:T(8,128)S(1)}, f32[16,128,128]{2,1,0:T(8,128)S(1)}, u32[]{:S(2)}, u32[]{:S(2)}) %collective-permute-start.15) | collective-permute-done | bytes 1048608 | tf_op jit(solution)/shard_map/ppermute | solution.py:411
  71.7 7.5 %update.1 = f32[36,128,128]{2,1,0:T(8,128)} custom-call(s32[3,36]{1,0:T(4,128)S(1)} %copy-done.16, f32[1,128,128]{2,1,0:T(8,128)S(1)} %copy-done.9, f32[1,128,128]{2,1,0:T(8,128)S(1)} %copy-done.15, f32[1,128,128]{2,1,0:T(8,128)S(1)} %copy-done.13, f32[1,128,128]{2,1,0:T(8,128)S(1)} %copy-done.11, f32[3,128,128]{2,1,0:T(8,128)S(1)} %copy-done.2, ...), custom_call_target="tpu_custom_call" | custom-call | tf_op jit(solution)/shard_map/update/pallas_call | solution.py:352
  (58 shorter events, 0.8 us)
Async XLA Ops:
  2.7 27.1 %copy-start.1 = (f32[3,128,128]{2,1,0:T(8,128)S(1)}, f32[3,128,128]{2,1,0:T(8,128)}, u32[]{:S(2)}) copy-start(f32[3,128,128]{2,1,0:T(8,128)} %get-tuple-element.31.refs_4_) | copy-start | bytes 589828
  2.7 9.8 %collective-permute-start.2 = (f32[1,128,128]{2,1,0:T(8,128)}, f32[1,128,128]{2,1,0:T(8,128)S(1)}, u32[]{:S(2)}, u32[]{:S(2)}) collective-permute-start(f32[1,128,128]{2,1,0:T(8,128)} %get-tuple-element.29.refs_0_), channel_id=1, source_target_pairs={{0,3},{1,2},{2,1},{3,0},{4,7},{5,6},{6,5},{7,4},{8,11},{9,10},{10,... | collective-permute-start | bytes 196616 | tf_op jit(solution)/shard_map/ppermute | solution.py:422
  6.1 6.3 %collective-permute-start.1 = (f32[1,128,128]{2,1,0:T(8,128)}, f32[1,128,128]{2,1,0:T(8,128)S(1)}, u32[]{:S(2)}, u32[]{:S(2)}) collective-permute-start(f32[1,128,128]{2,1,0:T(8,128)} %get-tuple-element.29.refs_0_), channel_id=1, source_target_pairs={{0,2},{1,3},{2,0},{3,1},{4,6},{5,7},{6,4},{7,5},{8,10},{9,11},{10,... | collective-permute-start | bytes 196616 | tf_op jit(solution)/shard_map/ppermute | solution.py:422
  6.1 6.3 %collective-permute-start = (f32[1,128,128]{2,1,0:T(8,128)}, f32[1,128,128]{2,1,0:T(8,128)S(1)}, u32[]{:S(2)}, u32[]{:S(2)}) collective-permute-start(f32[1,128,128]{2,1,0:T(8,128)} %get-tuple-element.29.refs_0_), channel_id=1, source_target_pairs={{0,1},{1,0},{2,3},{3,2},{4,5},{5,4},{6,7},{7,6},{8,9},{9,8},{10,11... | collective-permute-start | bytes 196616 | tf_op jit(solution)/shard_map/ppermute | solution.py:422
  6.5 10.0 %collective-permute-start.8 = (f32[3,128,128]{2,1,0:T(8,128)}, f32[3,128,128]{2,1,0:T(8,128)S(1)}, u32[]{:S(2)}, u32[]{:S(2)}) collective-permute-start(f32[3,128,128]{2,1,0:T(8,128)} %get-tuple-element.31.refs_4_), channel_id=1, source_target_pairs={{3,0},{6,5},{9,10},{12,15},{19,16},{22,21},{25,26},{28,31}} | collective-permute-start | bytes 589832 | tf_op jit(solution)/shard_map/ppermute | solution.py:422
  12.4 21.9 %copy-start.14 = (f32[1,128,128]{2,1,0:T(8,128)}, f32[1,128,128]{2,1,0:T(8,128)S(1)}, u32[]{:S(2)}) copy-start(f32[1,128,128]{2,1,0:T(8,128)S(1)} %collective-permute-done.refs_1_) | copy-start | bytes 196612
  12.5 21.9 %copy-start.12 = (f32[1,128,128]{2,1,0:T(8,128)}, f32[1,128,128]{2,1,0:T(8,128)S(1)}, u32[]{:S(2)}) copy-start(f32[1,128,128]{2,1,0:T(8,128)S(1)} %collective-permute-done.1.refs_2_) | copy-start | bytes 196612
  12.5 21.9 %copy-start.10 = (f32[1,128,128]{2,1,0:T(8,128)}, f32[1,128,128]{2,1,0:T(8,128)S(1)}, u32[]{:S(2)}) copy-start(f32[1,128,128]{2,1,0:T(8,128)S(1)} %collective-permute-done.2.refs_3_) | copy-start | bytes 196612
  12.5 10.6 %collective-permute-start.5 = (f32[4,128,128]{2,1,0:T(8,128)S(1)}, f32[4,128,128]{2,1,0:T(8,128)S(1)}, u32[]{:S(2)}, u32[]{:S(2)}) collective-permute-start(f32[4,128,128]{2,1,0:T(8,128)S(1)} %constant_dynamic-update-slice_fusion), channel_id=1, source_target_pairs={{0,24},{1,25},{2,26},{3,27},{4,28},{5,29},{6,30},{7,31},{8,16},{9,... | collective-permute-start | bytes 786440 | tf_op jit(solution)/shard_map/ppermute | solution.py:411
  13.8 15.3 %collective-permute-start.4 = (f32[4,128,128]{2,1,0:T(8,128)S(1)}, f32[4,128,128]{2,1,0:T(8,128)S(1)}, u32[]{:S(2)}, u32[]{:S(2)}) collective-permute-start(f32[4,128,128]{2,1,0:T(8,128)S(1)} %constant_dynamic-update-slice_fusion), channel_id=1, source_target_pairs={{0,16},{1,17},{2,18},{3,19},{4,20},{5,21},{6,22},{7,23},{8,24},{9,... | collective-permute-start | bytes 786440 | tf_op jit(solution)/shard_map/ppermute | solution.py:411
  15.1 14.0 %collective-permute-start.3 = (f32[4,128,128]{2,1,0:T(8,128)S(1)}, f32[4,128,128]{2,1,0:T(8,128)S(1)}, u32[]{:S(2)}, u32[]{:S(2)}) collective-permute-start(f32[4,128,128]{2,1,0:T(8,128)S(1)} %constant_dynamic-update-slice_fusion), channel_id=1, source_target_pairs={{0,8},{1,9},{2,10},{3,11},{4,12},{5,13},{6,14},{7,15},{8,0},{9,1},... | collective-permute-start | bytes 786440 | tf_op jit(solution)/shard_map/ppermute | solution.py:411
  15.8 3.2 %collective-permute-start.7 = (f32[3,128,128]{2,1,0:T(8,128)}, f32[3,128,128]{2,1,0:T(8,128)S(1)}, u32[]{:S(2)}, u32[]{:S(2)}) collective-permute-start(f32[3,128,128]{2,1,0:T(8,128)} %get-tuple-element.31.refs_4_), channel_id=1, source_target_pairs={{2,0},{7,5},{8,10},{13,15},{18,16},{23,21},{24,26},{29,31}} | collective-permute-start | bytes 589832 | tf_op jit(solution)/shard_map/ppermute | solution.py:422
  16.5 17.9 %copy-start.3 = (f32[3,128,128]{2,1,0:T(8,128)}, f32[3,128,128]{2,1,0:T(8,128)S(1)}, u32[]{:S(2)}) copy-start(f32[3,128,128]{2,1,0:T(8,128)S(1)} %collective-permute-done.8.refs_7_) | copy-start | bytes 589828
  16.5 6.7 %collective-permute-start.6 = (f32[3,128,128]{2,1,0:T(8,128)}, f32[3,128,128]{2,1,0:T(8,128)S(1)}, u32[]{:S(2)}, u32[]{:S(2)}) collective-permute-start(f32[3,128,128]{2,1,0:T(8,128)} %get-tuple-element.31.refs_4_), channel_id=1, source_target_pairs={{0,1},{1,0},{2,3},{3,2},{4,5},{5,4},{6,7},{7,6},{8,9},{9,8},{10,11... | collective-permute-start | bytes 589832 | tf_op jit(solution)/shard_map/ppermute | solution.py:422
  29.3 8.9 %collective-permute-start.14 = (f32[2,4,128,128]{3,2,1,0:T(8,128)S(1)}, f32[2,4,128,128]{3,2,1,0:T(8,128)S(1)}, u32[]{:S(2)}, u32[]{:S(2)}) collective-permute-start(f32[2,4,128,128]{3,2,1,0:T(8,128)S(1)} %pad_maximum_fusion.near), channel_id=1, source_target_pairs={{0,4},{1,5},{2,6},{3,7},{4,0},{5,1},{6,2},{7,3},{8,12},{9,13},{10,... | collective-permute-start | bytes 1572872 | tf_op jit(solution)/shard_map/ppermute | solution.py:411
  29.8 26.1 %collective-permute-start.13 = (f32[3,128,128]{2,1,0:T(8,128)S(1)}, f32[3,128,128]{2,1,0:T(8,128)S(1)}, u32[]{:S(2)}, u32[]{:S(2)}) collective-permute-start(f32[3,128,128]{2,1,0:T(8,128)S(1)} %copy-done.1), channel_id=1, source_target_pairs={{0,3},{1,2},{2,1},{4,7},{5,6},{7,4},{8,11},{10,9},{11,8},{13,14},{... | collective-permute-start | bytes 589832 | tf_op jit(solution)/shard_map/ppermute | solution.py:422
  31.1 24.8 %collective-permute-start.12 = (f32[3,128,128]{2,1,0:T(8,128)S(1)}, f32[3,128,128]{2,1,0:T(8,128)S(1)}, u32[]{:S(2)}, u32[]{:S(2)}) collective-permute-start(f32[3,128,128]{2,1,0:T(8,128)S(1)} %copy-done.1), channel_id=1, source_target_pairs={{0,2},{1,3},{3,1},{4,6},{5,7},{6,4},{9,11},{10,8},{11,9},{12,14},{... | collective-permute-start | bytes 589832 | tf_op jit(solution)/shard_map/ppermute | solution.py:422
  36.7 19.3 %collective-permute-start.11 = (f32[16,128,128]{2,1,0:T(8,128)}, f32[16,128,128]{2,1,0:T(8,128)S(1)}, u32[]{:S(2)}, u32[]{:S(2)}) collective-permute-start(f32[16,128,128]{2,1,0:T(8,128)} %pack.1), channel_id=1, source_target_pairs={{0,24},{5,29},{10,18},{15,23},{16,8},{21,13},{26,2},{31,7}} | collective-permute-start | bytes 3145736 | tf_op jit(solution)/shard_map/ppermute | solution.py:411
  37.4 18.6 %collective-permute-start.10 = (f32[16,128,128]{2,1,0:T(8,128)}, f32[16,128,128]{2,1,0:T(8,128)S(1)}, u32[]{:S(2)}, u32[]{:S(2)}) collective-permute-start(f32[16,128,128]{2,1,0:T(8,128)} %pack.1), channel_id=1, source_target_pairs={{0,16},{5,21},{10,26},{15,31},{16,0},{21,5},{26,10},{31,15}} | collective-permute-start | bytes 3145736 | tf_op jit(solution)/shard_map/ppermute | solution.py:411
  38.1 17.8 %collective-permute-start.9 = (f32[16,128,128]{2,1,0:T(8,128)}, f32[16,128,128]{2,1,0:T(8,128)S(1)}, u32[]{:S(2)}, u32[]{:S(2)}) collective-permute-start(f32[16,128,128]{2,1,0:T(8,128)} %pack.1), channel_id=1, source_target_pairs={{0,8},{5,13},{10,2},{15,7},{16,24},{21,29},{26,18},{31,23}} | collective-permute-start | bytes 3145736 | tf_op jit(solution)/shard_map/ppermute | solution.py:411
  56.0 15.6 %copy-start.9 = (f32[1,128,128]{2,1,0:T(8,128)S(1)}, f32[1,128,128]{2,1,0:T(8,128)}, u32[]{:S(2)}) copy-start(f32[1,128,128]{2,1,0:T(8,128)} %get-tuple-element.29.refs_0_) | copy-start | bytes 196612
  56.0 15.6 %copy-start.11 = (f32[1,128,128]{2,1,0:T(8,128)S(1)}, f32[1,128,128]{2,1,0:T(8,128)}, u32[]{:S(2)}) copy-start(f32[1,128,128]{2,1,0:T(8,128)} %copy-done.10) | copy-start | bytes 196612
  56.2 13.9 %collective-permute-start.16 = (f32[16,128,128]{2,1,0:T(8,128)S(1)}, f32[16,128,128]{2,1,0:T(8,128)S(1)}, u32[]{:S(2)}, u32[]{:S(2)}) collective-permute-start(f32[16,128,128]{2,1,0:T(8,128)S(1)} %broadcast_select_fusion.refs_11_), channel_id=1, source_target_pairs={{0,4},{2,6},{5,1},{7,3},{8,12},{10,14},{13,9},{15,11},{16,20},{18,... | collective-permute-start | bytes 3145736 | tf_op jit(solution)/shard_map/ppermute | solution.py:411
  57.9 13.7 %collective-permute-start.15 = (f32[16,128,128]{2,1,0:T(8,128)S(1)}, f32[16,128,128]{2,1,0:T(8,128)S(1)}, u32[]{:S(2)}, u32[]{:S(2)}) collective-permute-start(f32[16,128,128]{2,1,0:T(8,128)S(1)} %broadcast_select_fusion.1.refs_10_), channel_id=1, source_target_pairs={{0,4},{2,6},{5,1},{7,3},{8,12},{10,14},{13,9},{15,11},{16,20},{18,... | collective-permute-start | bytes 3145736 | tf_op jit(solution)/shard_map/ppermute | solution.py:411
  (11 other events, 152.4 us)

commit v2 on v1

v2 whole, which is shorter than its diff:
```python
import functools

import jax
import jax.numpy as jnp
from jax import lax
from jax.experimental import pallas as pl
from jax.experimental.pallas import tpu as pltpu
from jax.sharding import PartitionSpec as P

PANELS = 4
FIRST = 3
GROUP = 32
CHUNK = 16
SUB = 8
STRIPS = GROUP // SUB
F32 = jnp.float32
BF16 = jnp.bfloat16
HIGHEST = lax.Precision.HIGHEST
HBM = pl.BlockSpec(memory_space=pl.ANY)
SMEM = pl.BlockSpec(memory_space=pltpu.SMEM)
VMEM = pl.BlockSpec(memory_space=pltpu.VMEM)


def find(ids, rows, place, slots):
    me, column = lax.axis_index("row"), lax.axis_index("col")
    places = lax.broadcasted_iota(jnp.int32, (1, slots), 1)
    hit = (ids[1:2, :] == column) & (ids[0:1, :] == rows[place, me])
    return jnp.max(jnp.where(hit, places, -1))


def extract_kernel(col_devices, ids, rows, values, panel, head, table, sems):
    slots, count = values.shape[0], rows.shape[0]
    groups = rows.shape[1] // col_devices
    me = lax.axis_index("row")
    column = lax.axis_index("col")
    copies, present = [], []
    for place in range(count):
        found = find(ids, rows, place, slots)
        present.append(found >= 0)
        copy = pltpu.make_async_copy(
            values.at[jnp.maximum(found, 0)], panel.at[place], sems.at[place]
        )
        copy.start()
        copies.append(copy)
    row_ids, col_ids = ids[0:1, :], ids[1:2, :]
    row_place = jnp.full((1, slots), -1, jnp.int32)
    col_place = jnp.full((1, slots), -1, jnp.int32)
    for place in range(count):
        row_place = jnp.where(row_ids == rows[place, me], place, row_place)
        for group in range(groups):
            known = rows[place, column + group * col_devices]
            col_place = jnp.where(col_ids == known, group * count + place, col_place)
    both = (row_place >= 0) & (col_place >= 0)
    kind = jnp.where(row_ids < 0, 0, jnp.where(both, jnp.where(col_ids < PANELS, 2, 3), 1))
    table[0:1, :] = kind
    table[1:2, :] = jnp.maximum(row_place, 0)
    table[2:3, :] = jnp.maximum(col_place, 0)
    for place, copy in enumerate(copies):
        copy.wait()
        block = jnp.where(present[place], panel[place], 0.0)
        panel[place] = block
        if place == 0:
            head[0] = block


def extract(ids, rows, values, col_devices):
    slots, size, _ = values.shape
    count = rows.shape[0]
    return pl.pallas_call(
        functools.partial(extract_kernel, col_devices),
        name="extract",
        in_specs=[VMEM, SMEM, HBM],
        out_specs=[VMEM, VMEM, VMEM],
        out_shape=[
            jax.ShapeDtypeStruct((count, size, size), F32),
            jax.ShapeDtypeStruct((1, size, size), F32),
            jax.ShapeDtypeStruct((3, slots), jnp.int32),
        ],
        scratch_shapes=[pltpu.SemaphoreType.DMA((count,))],
    )(ids, rows, values)


def one_row(strip, place):
    return jnp.broadcast_to(strip[place : place + 1, :], strip.shape)


def eliminate(upper, extra, start):
    width = upper[0].shape[1]
    sublane = lax.broadcasted_iota(jnp.int32, (SUB, width), 0)
    scale = [jnp.zeros((SUB, width), F32)] * STRIPS
    for first in range(0, GROUP, CHUNK):
        chunk = range(first, first + CHUNK)
        cols = {
            t: {
                q: jnp.broadcast_to(upper[q][:, start + t : start + t + 1], (SUB, width))
                for q in range(t // SUB, STRIPS)
            }
            for t in chunk
        }
        for t in chunk:
            strip, place = divmod(t, SUB)
            pivot = one_row(cols[t][strip], place)
            reciprocal = 1.0 / pivot
            scale[strip] = jnp.where(sublane == place, lax.rsqrt(pivot), scale[strip])
            factor = {q: cols[t][q] * reciprocal for q in range(strip, STRIPS)}
            factor[strip] = jnp.where(sublane > place, factor[strip], 0.0)
            for u in chunk[t + 1 - first :]:
                entry = one_row(cols[t][u // SUB], u % SUB)
                for q in range(u // SUB, STRIPS):
                    cols[u][q] = cols[u][q] - factor[q] * entry
            pivot_upper = one_row(upper[strip], place)
            pivot_extra = one_row(extra[strip], place)
            for q in range(strip, STRIPS):
                upper[q] = upper[q] - factor[q] * pivot_upper
                extra[q] = extra[q] - factor[q] * pivot_extra
    upper = jnp.concatenate([upper[q] * scale[q] for q in range(STRIPS)], axis=0)
    extra = jnp.concatenate([extra[q] * scale[q] for q in range(STRIPS)], axis=0)
    return upper, extra


def exact(a, b):
    return jnp.dot(a, b, precision=HIGHEST, preferred_element_type=F32)


def exact_t(a, b):
    return lax.dot_general(
        a, b, (((1,), (1,)), ((), ())), precision=HIGHEST, preferred_element_type=F32
    )


def factor_block(block, work, extra_work):
    size = block.shape[0]
    row_place = lax.broadcasted_iota(jnp.int32, (size, size), 0)
    col_place = lax.broadcasted_iota(jnp.int32, (size, size), 1)
    work[...] = block
    extra_work[...] = jnp.where(row_place == col_place, 1.0, 0.0)
    uppers, extras = [], []
    for start in range(0, size, GROUP):
        strips = [pl.ds(start + q * SUB, SUB) for q in range(STRIPS)]
        upper = [work[s, :] for s in strips]
        extra = [extra_work[s, :] for s in strips]
        upper, extra = eliminate(upper, extra, start)
        uppers.append(upper)
        extras.append(extra)
        end = start + GROUP
        if end < size:
            left = upper[:, end:].T
            work[end:, :] = work[end:, :] - exact(left, upper)
            extra_work[end:, :] = extra_work[end:, :] - exact(left, extra)
    upper = jnp.concatenate(uppers, axis=0)
    inverse = jnp.where(row_place >= col_place, jnp.concatenate(extras, axis=0), 0.0)
    return jnp.where(row_place <= col_place, upper, 0.0), inverse


def halves(x):
    high = x.astype(BF16)
    return high, (x - high.astype(F32)).astype(BF16)


def at(row, col):
    return row * (row + 1) // 2 + col


def factor_steps(steps, lead, inverse, work, extra_work):
    for k in steps:
        upper, inv = factor_block(lead[at(k, k)], work, extra_work)
        lead[at(k, k)] = upper.T
        for i in range(k + 1, PANELS):
            lead[at(i, k)] = exact_t(lead[at(i, k)], inv)
        for i in range(k + 1, PANELS):
            for j in range(k + 1, i + 1):
                lead[at(i, j)] = lead[at(i, j)] - exact_t(lead[at(i, k)], lead[at(j, k)])
        inverse[at(k, k)] = inv
        for j in range(k):
            total = exact(lead[at(k, j)], inverse[at(j, j)])
            for m in range(j + 1, k):
                total = total + exact(lead[at(k, m)], inverse[at(m, j)])
            inverse[at(k, j)] = -exact(inv, total)


def first_kernel(near, across, lead, inverse, work, extra_work):
    me = lax.axis_index("row")
    column = lax.axis_index("col")
    for row in range(PANELS):
        for col in range(row + 1):
            flip_x = ((me // 2) % 2) ^ (row // 2)
            flip_core = (me % 2) ^ (row % 2)
            place = column ^ col

            @pl.when(flip_core == 0)
            def _():
                lead[at(row, col)] = near[flip_x, place]

            @pl.when(flip_core == 1)
            def _():
                lead[at(row, col)] = across[flip_x, place]

    factor_steps(range(FIRST), lead, inverse, work, extra_work)


def second_kernel(
    lead_in, inverse_in, factor, inv_hi, inv_lo, lead, inverse, work, extra_work
):
    size = work.shape[0]
    done = at(FIRST, 0)
    lead[...] = lead_in[...]
    inverse[:done] = inverse_in[...]
    factor_steps(range(FIRST, PANELS), lead, inverse, work, extra_work)
    zero = jnp.zeros((size, size), BF16)
    for i in range(PANELS):
        for j in range(PANELS):
            rows, cols = slice(i * size, (i + 1) * size), slice(j * size, (j + 1) * size)
            hi, lo = halves(inverse[at(i, j)]) if j <= i else (zero, zero)
            inv_hi[rows, cols], inv_lo[rows, cols] = hi, lo
    row = jnp.minimum(lax.axis_index("row"), PANELS - 1)
    factor[...] = lead[at(row, jnp.minimum(lax.axis_index("col"), row))]


FACTOR_COST = pl.CostEstimate(flops=2**33, bytes_accessed=2**24, transcendentals=0)


def factor_first(near, across):
    size = near.shape[-1]
    return pl.pallas_call(
        first_kernel,
        name="factor_first",
        in_specs=[VMEM, VMEM],
        out_specs=[VMEM, VMEM],
        out_shape=[
            jax.ShapeDtypeStruct((at(PANELS, 0), size, size), F32),
            jax.ShapeDtypeStruct((at(FIRST, 0), size, size), F32),
        ],
        scratch_shapes=[pltpu.VMEM((size, size), F32), pltpu.VMEM((size, size), F32)],
        compiler_params=pltpu.CompilerParams(vmem_limit_bytes=16 * 2**20),
        cost_estimate=FACTOR_COST,
    )(near, across)


def factor_second(lead, inverse):
    size = lead.shape[-1]
    width = PANELS * size
    return pl.pallas_call(
        second_kernel,
        name="factor_second",
        in_specs=[VMEM, VMEM],
        out_specs=[VMEM, VMEM, VMEM],
        out_shape=[
            jax.ShapeDtypeStruct((size, size), F32),
            jax.ShapeDtypeStruct((width, width), BF16),
            jax.ShapeDtypeStruct((width, width), BF16),
        ],
        scratch_shapes=[
            pltpu.VMEM((at(PANELS, 0), size, size), F32),
            pltpu.VMEM((at(PANELS, 0), size, size), F32),
            pltpu.VMEM((size, size), F32),
            pltpu.VMEM((size, size), F32),
        ],
        compiler_params=pltpu.CompilerParams(vmem_limit_bytes=16 * 2**20),
        cost_estimate=FACTOR_COST,
    )(lead, inverse)


def dot3_t(a, b):
    dims = (((1,), (1,)), ((), ()))
    dot = functools.partial(lax.dot_general, dimension_numbers=dims, preferred_element_type=F32)
    return dot(a[0], b[0]) + (dot(a[0], b[1]) + dot(a[1], b[0]))


def spread(column, place):
    return place ^ (2 * (column % 2))


def update_kernel(plan, table, *refs):
    row_devices, count, col_devices = plan
    groups = row_devices // col_devices
    refs = list(refs)
    panels = [refs.pop(0) for _ in range(col_devices)]
    near = [refs.pop(0) for _ in range(row_devices // 2)]
    across = refs.pop(0)
    factor, inv_hi, inv_lo, values, out = [refs.pop(0) for _ in range(5)]
    raw, high, low, product, column_blocks, slots_in, sems, io_sems = refs
    slots, size, _ = values.shape
    own_rows = count * size
    far_rows = groups * own_rows
    me = lax.axis_index("row")
    column = lax.axis_index("col")

    load = pltpu.make_async_copy(values, slots_in, io_sems.at[0])
    load.start()
    twice = (me ^ column) % col_devices == 0
    for p in range(col_devices):
        col = column ^ p

        @pl.when((col < PANELS) & jnp.logical_not(twice))
        def _():
            lanes = pl.ds(pl.multiple_of(jnp.minimum(col, PANELS - 1) * size, size), size)
            for place in range(count):
                pltpu.make_async_copy(
                    panels[p].at[place], raw.at[pl.ds(place * size, size), lanes], sems.at[0]
                ).start()

    for flip in range(row_devices):
        holder = me ^ flip
        group, col = holder // col_devices, spread(column, holder % col_devices)

        @pl.when(col < PANELS)
        def _():
            lanes = pl.ds(pl.multiple_of(jnp.minimum(col, PANELS - 1) * size, size), size)
            for place in range(count):
                if flip % 2 == 0:
                    source = near[flip // 2].at[place]
                else:
                    source = across.at[flip // 2 * count + place]
                start = pl.multiple_of(own_rows + (group * count + place) * size, size)
                pltpu.make_async_copy(
                    source, raw.at[pl.ds(start, size), lanes], sems.at[1]
                ).start()

                @pl.when(twice & (group == me // col_devices))
                def _():
                    pltpu.make_async_copy(
                        source, raw.at[pl.ds(place * size, size), lanes], sems.at[0]
                    ).start()

    half = PANELS * size // 2
    for part in range(groups + 1):
        if part < 2:
            arrived = raw.at[:own_rows, :] if part == 0 else raw.at[own_rows:, :]
            pltpu.make_async_copy(arrived, arrived, sems.at[part]).wait()
        rows = pl.ds(part * own_rows, own_rows)
        hi, lo = halves(raw[rows, :])
        first = dot3_t(
            (hi[:, :half], lo[:, :half]), (inv_hi[:half, :half], inv_lo[:half, :half])
        )
        second = dot3_t((hi, lo), (inv_hi[half:, :], inv_lo[half:, :]))
        if part == 0:
            raw[rows, :half], raw[rows, half:] = first, second
        high[rows, :half], low[rows, :half] = halves(first)
        high[rows, half:], low[rows, half:] = halves(second)
    load.wait()
    own = pl.ds(0, own_rows)
    for start in range(0, far_rows, 2 * size):
        rows = pl.ds(own_rows + start, 2 * size)
        result = dot3_t((high[own, :], low[own, :]), (high[rows, :], low[rows, :]))
        for place in range(count):
            for side in range(2):
                product[place, start // size + side] = result[
                    place * size : (place + 1) * size, side * size : (side + 1) * size
                ]
    lanes = pl.ds(pl.multiple_of(jnp.minimum(column, PANELS - 1) * size, size), size)
    for place in range(count):
        solved_block = raw[place * size : (place + 1) * size, lanes]
        if place == 0:
            solved_block = jnp.where(me < PANELS, factor[...], solved_block)
        column_blocks[place] = solved_block

    def finish(slot, carry):
        kind, row, col = table[0, slot], table[1, slot], table[2, slot]
        old = slots_in[slot]
        new = jnp.where(kind == 3, old - product[row, col], jnp.where(kind == 1, old, 0.0))
        slots_in[slot] = jnp.where(kind == 2, column_blocks[row], new)
        pltpu.make_async_copy(slots_in.at[slot], out.at[slot], io_sems.at[1]).start()
        return carry

    lax.fori_loop(0, slots, finish, 0, unroll=4)
    pltpu.make_async_copy(slots_in, out, io_sems.at[1]).wait()


def update(table, panels, near, across, solved_lead, values, row_devices):
    slots, size, _ = values.shape
    col_devices, count = len(panels), panels[0].shape[0]
    groups = row_devices // col_devices
    flat = [*panels, *near, across]
    width = PANELS * size
    rows = (groups + 1) * count * size
    return pl.pallas_call(
        functools.partial(update_kernel, (row_devices, count, col_devices)),
        name="update",
        in_specs=[SMEM] + [HBM] * len(flat) + [VMEM, VMEM, VMEM, HBM],
        out_specs=HBM,
        out_shape=jax.ShapeDtypeStruct(values.shape, F32),
        scratch_shapes=[
            pltpu.VMEM((rows, width), F32),
            pltpu.VMEM((rows, width), BF16),
            pltpu.VMEM((rows, width), BF16),
            pltpu.VMEM((count, groups * count, size, size), F32),
            pltpu.VMEM((count, size, size), F32),
            pltpu.VMEM((slots, size, size), F32),
            pltpu.SemaphoreType.DMA((2,)),
            pltpu.SemaphoreType.DMA((2,)),
        ],
        compiler_params=pltpu.CompilerParams(vmem_limit_bytes=24 * 2**20),
    )(table, *flat, *solved_lead, values)


def body(values, block_ids, coupled_rows):
    row_devices, col_devices = lax.axis_size("row"), lax.axis_size("col")
    every_row, every_col = range(row_devices), range(col_devices)
    me = lax.axis_index("row")
    slot_values = values[0, 0]
    rows = coupled_rows.T

    def send(x, flip, keep=lambda r, c: True):
        pairs = [
            (r * col_devices + c, (r ^ flip) * col_devices + c)
            for r in every_row
            for c in every_col
            if keep(r, c)
        ]
        return lax.ppermute(x, ("row", "col"), pairs)

    def over_col(x, keep=lambda r, c: True):
        got = [x]
        for p in range(1, col_devices):
            pairs = [
                (r * col_devices + c, r * col_devices + (c ^ p))
                for r in every_row
                for c in range(PANELS)
                if keep(r, c ^ p)
            ]
            got.append(lax.ppermute(x, ("row", "col"), pairs))
        return got

    panel, head, table = extract(block_ids[0, 0].T, rows, slot_values, col_devices)

    block = jnp.where(me < PANELS, head, 0.0)
    step = PANELS
    while step < row_devices:
        block = block + send(block, step, lambda r, c: r < step)
        step *= 2
    blocks = over_col(block)

    pairs = [
        ((q + a) * col_devices + b, (q + spread(a, b)) * col_devices + a)
        for q in range(0, row_devices, col_devices)
        for a in every_col
        for b in range(PANELS)
    ]
    blocks, panel = lax.optimization_barrier((blocks, panel))
    turned = lax.ppermute(panel, ("row", "col"), pairs)

    panels = over_col(panel, lambda r, c: (r ^ c) % col_devices != 0)

    mine = jnp.concatenate(blocks, axis=0)
    beside, turned, panels[1] = lax.optimization_barrier((send(mine, 2), turned, panels[1]))
    near_lead = jnp.stack([mine, beside])
    across_lead = send(near_lead, 1)
    near = [turned if flip == 0 else send(turned, flip) for flip in range(0, row_devices, 2)]
    begun = factor_first(near_lead, across_lead)
    near, panels[2:], begun = lax.optimization_barrier((near, panels[2:], begun))
    across = send(jnp.concatenate(near, axis=0), 1)
    solved_lead = factor_second(*begun)

    result = update(table, panels, near, across, solved_lead, slot_values, row_devices)
    return result[None, None]


def solution(mesh):
    placed = (P("row", "col", None, None, None), P("row", "col", None, None), P())
    return jax.shard_map(
        body,
        mesh=mesh,
        in_specs=placed,
        out_specs=P("row", "col", None, None, None),
        check_vma=False,
    )
```

time: 79.8 us -> 75.2 us (0.942)
  Pallas kernels: 29.5 us -> 26.5 us
  starting transfers between devices: 25.3 us -> 22.5 us
  waiting for transfers between devices: 22.6 us -> 24.7 us
  local copies, waits for them, and re-layouts: 0.95 us -> 0.04 us
    ppermute x9 -> x7, waiting for transfers between devices: 18.4 us -> 3.73 us  [send(): return lax.ppermute(x, ('row', 'col'), pairs)]
    ppermute x0 -> x1, waiting for transfers between devices: none -> 10.1 us  [body(): turned = lax.ppermute(panel, ('row', 'col'), pairs)]
    ppermute x8 -> x6, starting transfers between devices: 16.5 us -> 8.86 us  [over_col(): got.append(lax.ppermute(x, ('row', 'col'), pairs))]
    ppermute x8 -> x6, waiting for transfers between devices: 4.16 us -> 10.9 us  [over_col(): got.append(lax.ppermute(x, ('row', 'col'), pairs))]
    ppermute x0 -> x1, starting transfers between devices: none -> 5.12 us  [body(): turned = lax.ppermute(panel, ('row', 'col'), pairs)]
    pallas_call x3, Pallas kernels: 26.8 us -> 23.7 us  [the longest x1 12.6 us: factor_first(): pl.pallas_call(first_kernel, name='factor_first', in_specs=[VMEM, VMEM],...]
    unnamed x39 -> x9, local copies, waits for them, and re-layouts: 0.94 us -> 0.04 us
    ppermute x9 -> x7, starting transfers between devices: 8.85 us -> 8.57 us  [send(): return lax.ppermute(x, ('row', 'col'), pairs)]
  transfers between devices with their start and end apart: 17 -> 14, of which waited for: 4 -> 6; matrix products, arithmetic and copies ran while one was open for 1% -> 0% of each run, Pallas kernels for 24% -> 22%
where the time goes in v2:
time: 75.2 us; the launch traced here: 74.3 us
  Pallas kernels  26.5 us (35%)
  waiting for transfers between devices  24.7 us (33%)
  starting transfers between devices  22.5 us (30%)
    pallas_call x1, Pallas kernels, factor_first(): pl.pallas_call(first_kernel, name='factor_first', in_specs=[VMEM, VMEM],...  12.6 us
    ppermute x6, waiting for transfers between devices, over_col(): got.append(lax.ppermute(x, ('row', 'col'), pairs))  10.9 us
    ppermute x1, waiting for transfers between devices, body(): turned = lax.ppermute(panel, ('row', 'col'), pairs)  10.1 us
    ppermute x6, starting transfers between devices, over_col(): got.append(lax.ppermute(x, ('row', 'col'), pairs))  8.86 us
    ppermute x7, starting transfers between devices, send(): return lax.ppermute(x, ('row', 'col'), pairs)  8.57 us
    pallas_call x1, Pallas kernels, update(): pl.pallas_call(functools.partial(update_kernel, (row_devices, count, col_...  7.13 us
    ppermute x1, starting transfers between devices, body(): turned = lax.ppermute(panel, ('row', 'col'), pairs)  5.12 us
    pallas_call x1, Pallas kernels, factor_second(): pl.pallas_call(second_kernel, name='factor_second', in_specs=[VMEM, VMEM]...  4.06 us
  transfers between devices with their start and end apart: 14, of which 6 were waited for; matrix products, arithmetic and copies ran while one was open for 0% of the time, Pallas kernels for 22%

profile of v2, /device:TPU:7, one launch (start us, length us, event | category | flops | bytes accessed | tf_op | source)
XLA Modules:
  0.0 74.3 jit_solution(5234337862240352648)
XLA Ops:
  0.0 2.7 %extract.1 = (f32[4,128,128]{2,1,0:T(8,128)}, f32[1,128,128]{2,1,0:T(8,128)}, s32[3,36]{1,0:T(4,128)}) custom-call(s32[2,36]{1,0:T(2,128)} %bitcast.13, s32[4,8]{1,0:T(4,128)} %bitcast.12, f32[36,128,128]{2,1,0:T(8,128)} %bitcast.8), custom_call_target="tpu_custom_call" | custom-call | tf_op jit(solution)/shard_map/extract/pallas_call | solution.py:69
  2.8 1.3 %collective-permute-start = (f32[1,128,128]{2,1,0:T(8,128)S(1)}, f32[1,128,128]{2,1,0:T(8,128)S(1)}, u32[]{:S(2)}, u32[]{:S(2)}) collective-permute-start(f32[1,128,128]{2,1,0:T(8,128)S(1)} %broadcast_select_fusion), channel_id=1, source_target_pairs={{0,16},{1,17},{2,18},{3,19},{4,20},{5,21},{6,22},{7,23},{8,24},{9,... | collective-permute-start | bytes 196616 | tf_op jit(solution)/shard_map/ppermute | solution.py:410
  4.1 3.7 %collective-permute-done = f32[1,128,128]{2,1,0:T(8,128)S(1)} collective-permute-done((f32[1,128,128]{2,1,0:T(8,128)S(1)}, f32[1,128,128]{2,1,0:T(8,128)S(1)}, u32[]{:S(2)}, u32[]{:S(2)}) %collective-permute-start) | collective-permute-done | bytes 65568 | tf_op jit(solution)/shard_map/ppermute | solution.py:410
  7.8 3.4 %collective-permute-start.3 = (f32[1,128,128]{2,1,0:T(8,128)S(1)}, f32[1,128,128]{2,1,0:T(8,128)S(1)}, u32[]{:S(2)}, u32[]{:S(2)}) collective-permute-start(f32[1,128,128]{2,1,0:T(8,128)S(1)} %fusion), channel_id=1, source_target_pairs={{0,3},{1,2},{2,1},{3,0},{4,7},{5,6},{6,5},{7,4},{8,11},{9,10},{10,... | collective-permute-start | bytes 196616 | tf_op jit(solution)/shard_map/ppermute | solution.py:421
  11.2 0.4 collective-permute-start.1
  11.5 1.3 %collective-permute-done.3 = f32[1,128,128]{2,1,0:T(8,128)S(1)} collective-permute-done((f32[1,128,128]{2,1,0:T(8,128)S(1)}, f32[1,128,128]{2,1,0:T(8,128)S(1)}, u32[]{:S(2)}, u32[]{:S(2)}) %collective-permute-start.3) | collective-permute-done | bytes 65568 | tf_op jit(solution)/shard_map/ppermute | solution.py:421
  12.8 3.8 %collective-permute-done.2 = f32[1,128,128]{2,1,0:T(8,128)S(1)} collective-permute-done((f32[1,128,128]{2,1,0:T(8,128)S(1)}, f32[1,128,128]{2,1,0:T(8,128)S(1)}, u32[]{:S(2)}, u32[]{:S(2)}) %collective-permute-start.2) | collective-permute-done | bytes 65568 | tf_op jit(solution)/shard_map/ppermute | solution.py:421
  16.7 0.3 collective-permute-start.4
  17.0 1.9 %collective-permute-start.6 = (f32[4,128,128]{2,1,0:T(8,128)}, f32[4,128,128]{2,1,0:T(8,128)S(1)}, u32[]{:S(2)}, u32[]{:S(2)}) collective-permute-start(f32[4,128,128]{2,1,0:T(8,128)} %get-tuple-element.32.refs_0_), channel_id=1, source_target_pairs={{0,1},{2,3},{3,2},{5,4},{6,7},{7,6},{8,9},{9,8},{10,11},{12,13},{1... | collective-permute-start | bytes 786440 | tf_op jit(solution)/shard_map/ppermute | solution.py:421
  18.9 5.1 %collective-permute-start.5 = (f32[4,128,128]{2,1,0:T(8,128)}, f32[4,128,128]{2,1,0:T(8,128)S(1)}, u32[]{:S(2)}, u32[]{:S(2)}) collective-permute-start(f32[4,128,128]{2,1,0:T(8,128)} %get-tuple-element.32.refs_0_), channel_id=1, source_target_pairs={{0,0},{1,4},{2,8},{3,12},{4,9},{5,13},{6,1},{7,5},{8,2},{9,6},{10,... | collective-permute-start | bytes 786440 | tf_op jit(solution)/shard_map/ppermute | solution.py:440
  24.1 0.7 collective-permute-done.6.refs_1_
  24.8 10.1 %collective-permute-done.5.refs_4_ = f32[4,128,128]{2,1,0:T(8,128)S(1)} collective-permute-done((f32[4,128,128]{2,1,0:T(8,128)}, f32[4,128,128]{2,1,0:T(8,128)S(1)}, u32[]{:S(2)}, u32[]{:S(2)}) %collective-permute-start.5) | collective-permute-done | bytes 262176 | tf_op jit(solution)/shard_map/ppermute | solution.py:440
  34.9 2.8 %collective-permute-start.12 = (f32[2,4,128,128]{3,2,1,0:T(8,128)S(1)}, f32[2,4,128,128]{3,2,1,0:T(8,128)S(1)}, u32[]{:S(2)}, u32[]{:S(2)}) collective-permute-start(f32[2,4,128,128]{3,2,1,0:T(8,128)S(1)} %pad_maximum_fusion.1.near), channel_id=1, source_target_pairs={{0,4},{1,5},{2,6},{3,7},{4,0},{5,1},{6,2},{7,3},{8,12},{9,13},{10,... | collective-permute-start | bytes 1572872 | tf_op jit(solution)/shard_map/ppermute | solution.py:410
  37.7 1.3 %collective-permute-start.11 = (f32[4,128,128]{2,1,0:T(8,128)}, f32[4,128,128]{2,1,0:T(8,128)S(1)}, u32[]{:S(2)}, u32[]{:S(2)}) collective-permute-start(f32[4,128,128]{2,1,0:T(8,128)} %get-tuple-element.32.refs_0_), channel_id=1, source_target_pairs={{0,3},{1,2},{2,1},{4,7},{5,6},{7,4},{8,11},{10,9},{11,8},{13,14},{... | collective-permute-start | bytes 786440 | tf_op jit(solution)/shard_map/ppermute | solution.py:421
  39.0 1.9 %collective-permute-start.10 = (f32[4,128,128]{2,1,0:T(8,128)}, f32[4,128,128]{2,1,0:T(8,128)S(1)}, u32[]{:S(2)}, u32[]{:S(2)}) collective-permute-start(f32[4,128,128]{2,1,0:T(8,128)} %get-tuple-element.32.refs_0_), channel_id=1, source_target_pairs={{0,2},{1,3},{3,1},{4,6},{5,7},{6,4},{9,11},{10,8},{11,9},{12,14},{... | collective-permute-start | bytes 786440 | tf_op jit(solution)/shard_map/ppermute | solution.py:421
  40.9 2.3 %collective-permute-start.9 = (f32[4,128,128]{2,1,0:T(8,128)S(1)}, f32[4,128,128]{2,1,0:T(8,128)S(1)}, u32[]{:S(2)}, u32[]{:S(2)}) collective-permute-start(f32[4,128,128]{2,1,0:T(8,128)S(1)} %collective-permute-done.5.refs_4_), channel_id=1, source_target_pairs={{0,24},{1,25},{2,26},{3,27},{4,28},{5,29},{6,30},{7,31},{8,16},{9,... | collective-permute-start | bytes 786440 | tf_op jit(solution)/shard_map/ppermute | solution.py:410
  43.3 1.0 %collective-permute-start.8 = (f32[4,128,128]{2,1,0:T(8,128)S(1)}, f32[4,128,128]{2,1,0:T(8,128)S(1)}, u32[]{:S(2)}, u32[]{:S(2)}) collective-permute-start(f32[4,128,128]{2,1,0:T(8,128)S(1)} %collective-permute-done.5.refs_4_), channel_id=1, source_target_pairs={{0,16},{1,17},{2,18},{3,19},{4,20},{5,21},{6,22},{7,23},{8,24},{9,... | collective-permute-start | bytes 786440 | tf_op jit(solution)/shard_map/ppermute | solution.py:410
  44.2 12.6 %factor_first.1 = (f32[10,128,128]{2,1,0:T(8,128)S(1)}, f32[6,128,128]{2,1,0:T(8,128)S(1)}) custom-call(f32[2,4,128,128]{3,2,1,0:T(8,128)S(1)} %pad_maximum_fusion.1.near, f32[2,4,128,128]{3,2,1,0:T(8,128)S(1)} %collective-permute-done.12.across), custom_call_target="tpu_custom_call" | custom-call | flops 8589934592 | bytes 16777216 | tf_op jit(solution)/shard_map/factor_first/pallas_call | solution.py:224
  56.8 5.1 %collective-permute-done.10.refs_2_ = f32[4,128,128]{2,1,0:T(8,128)S(1)} collective-permute-done((f32[4,128,128]{2,1,0:T(8,128)}, f32[4,128,128]{2,1,0:T(8,128)S(1)}, u32[]{:S(2)}, u32[]{:S(2)}) %collective-permute-start.10) | collective-permute-done | bytes 262176 | tf_op jit(solution)/shard_map/ppermute | solution.py:421
  61.9 0.1 pad_maximum_fusion
  62.0 0.0 copy-start
  62.0 0.9 %collective-permute-start.13 = (f32[16,128,128]{2,1,0:T(8,128)S(1)}, f32[16,128,128]{2,1,0:T(8,128)S(1)}, u32[]{:S(2)}, u32[]{:S(2)}) collective-permute-start(f32[16,128,128]{2,1,0:T(8,128)S(1)} %pad_maximum_fusion), channel_id=1, source_target_pairs={{0,4},{1,5},{2,6},{3,7},{4,0},{5,1},{6,2},{7,3},{8,12},{9,13},{10,... | collective-permute-start | bytes 3145736 | tf_op jit(solution)/shard_map/ppermute | solution.py:410
  62.9 4.1 %factor_second.1 = (f32[128,128]{1,0:T(8,128)S(1)}, bf16[512,512]{1,0:T(8,128)(2,1)S(1)}, bf16[512,512]{1,0:T(8,128)(2,1)S(1)}) custom-call(f32[10,128,128]{2,1,0:T(8,128)S(1)} %get-tuple-element.48.lead_in, f32[6,128,128]{2,1,0:T(8,128)S(1)} %get-tuple-element.49.inverse_in), custom_call_target="tpu_custom_call" | custom-call | flops 8589934592 | bytes 16777216 | tf_op jit(solution)/shard_map/factor_second/pallas_call | solution.py:242
  67.0 7.1 %update.1 = f32[36,128,128]{2,1,0:T(8,128)} custom-call(s32[3,36]{1,0:T(4,128)S(1)} %copy-done.2, f32[4,128,128]{2,1,0:T(8,128)S(1)} %copy-done.1, f32[4,128,128]{2,1,0:T(8,128)S(1)} %collective-permute-done.6.refs_1_, f32[4,128,128]{2,1,0:T(8,128)S(1)} %collective-permute-done.10.refs_2_, f32[4,128,128]{2,1,0:T(8,128)S(1)} %collective-permute-done.11.refs_3_, ...), custom_call_target="tpu_custom_call" | custom-call | tf_op jit(solution)/shard_map/update/pallas_call | solution.py:376
  (22 shorter events, 0.1 us)
Async XLA Ops:
  2.8 5.0 %collective-permute-start = (f32[1,128,128]{2,1,0:T(8,128)S(1)}, f32[1,128,128]{2,1,0:T(8,128)S(1)}, u32[]{:S(2)}, u32[]{:S(2)}) collective-permute-start(f32[1,128,128]{2,1,0:T(8,128)S(1)} %broadcast_select_fusion), channel_id=1, source_target_pairs={{0,16},{1,17},{2,18},{3,19},{4,20},{5,21},{6,22},{7,23},{8,24},{9,... | collective-permute-start | bytes 196616 | tf_op jit(solution)/shard_map/ppermute | solution.py:410
  7.8 5.0 %collective-permute-start.3 = (f32[1,128,128]{2,1,0:T(8,128)S(1)}, f32[1,128,128]{2,1,0:T(8,128)S(1)}, u32[]{:S(2)}, u32[]{:S(2)}) collective-permute-start(f32[1,128,128]{2,1,0:T(8,128)S(1)} %fusion), channel_id=1, source_target_pairs={{0,3},{1,2},{2,1},{3,0},{4,7},{5,6},{6,5},{7,4},{8,11},{9,10},{10,... | collective-permute-start | bytes 196616 | tf_op jit(solution)/shard_map/ppermute | solution.py:421
  11.2 5.4 %collective-permute-start.2 = (f32[1,128,128]{2,1,0:T(8,128)S(1)}, f32[1,128,128]{2,1,0:T(8,128)S(1)}, u32[]{:S(2)}, u32[]{:S(2)}) collective-permute-start(f32[1,128,128]{2,1,0:T(8,128)S(1)} %fusion), channel_id=1, source_target_pairs={{0,2},{1,3},{2,0},{3,1},{4,6},{5,7},{6,4},{7,5},{8,10},{9,11},{10,... | collective-permute-start | bytes 196616 | tf_op jit(solution)/shard_map/ppermute | solution.py:421
  11.2 5.4 %collective-permute-start.1 = (f32[1,128,128]{2,1,0:T(8,128)S(1)}, f32[1,128,128]{2,1,0:T(8,128)S(1)}, u32[]{:S(2)}, u32[]{:S(2)}) collective-permute-start(f32[1,128,128]{2,1,0:T(8,128)S(1)} %fusion), channel_id=1, source_target_pairs={{0,1},{1,0},{2,3},{3,2},{4,5},{5,4},{6,7},{7,6},{8,9},{9,8},{10,11... | collective-permute-start | bytes 196616 | tf_op jit(solution)/shard_map/ppermute | solution.py:421
  16.7 7.4 %collective-permute-start.4 = (f32[4,128,128]{2,1,0:T(8,128)S(1)}, f32[4,128,128]{2,1,0:T(8,128)S(1)}, u32[]{:S(2)}, u32[]{:S(2)}) collective-permute-start(f32[4,128,128]{2,1,0:T(8,128)S(1)} %constant_dynamic-update-slice_fusion), channel_id=1, source_target_pairs={{0,8},{1,9},{2,10},{3,11},{4,12},{5,13},{6,14},{7,15},{8,0},{9,1},... | collective-permute-start | bytes 786440 | tf_op jit(solution)/shard_map/ppermute | solution.py:410
  17.0 7.8 %collective-permute-start.6 = (f32[4,128,128]{2,1,0:T(8,128)}, f32[4,128,128]{2,1,0:T(8,128)S(1)}, u32[]{:S(2)}, u32[]{:S(2)}) collective-permute-start(f32[4,128,128]{2,1,0:T(8,128)} %get-tuple-element.32.refs_0_), channel_id=1, source_target_pairs={{0,1},{2,3},{3,2},{5,4},{6,7},{7,6},{8,9},{9,8},{10,11},{12,13},{1... | collective-permute-start | bytes 786440 | tf_op jit(solution)/shard_map/ppermute | solution.py:421
  18.9 16.0 %collective-permute-start.5 = (f32[4,128,128]{2,1,0:T(8,128)}, f32[4,128,128]{2,1,0:T(8,128)S(1)}, u32[]{:S(2)}, u32[]{:S(2)}) collective-permute-start(f32[4,128,128]{2,1,0:T(8,128)} %get-tuple-element.32.refs_0_), channel_id=1, source_target_pairs={{0,0},{1,4},{2,8},{3,12},{4,9},{5,13},{6,1},{7,5},{8,2},{9,6},{10,... | collective-permute-start | bytes 786440 | tf_op jit(solution)/shard_map/ppermute | solution.py:440
  34.9 9.3 %collective-permute-start.12 = (f32[2,4,128,128]{3,2,1,0:T(8,128)S(1)}, f32[2,4,128,128]{3,2,1,0:T(8,128)S(1)}, u32[]{:S(2)}, u32[]{:S(2)}) collective-permute-start(f32[2,4,128,128]{3,2,1,0:T(8,128)S(1)} %pad_maximum_fusion.1.near), channel_id=1, source_target_pairs={{0,4},{1,5},{2,6},{3,7},{4,0},{5,1},{6,2},{7,3},{8,12},{9,13},{10,... | collective-permute-start | bytes 1572872 | tf_op jit(solution)/shard_map/ppermute | solution.py:410
  37.7 19.0 %collective-permute-start.11 = (f32[4,128,128]{2,1,0:T(8,128)}, f32[4,128,128]{2,1,0:T(8,128)S(1)}, u32[]{:S(2)}, u32[]{:S(2)}) collective-permute-start(f32[4,128,128]{2,1,0:T(8,128)} %get-tuple-element.32.refs_0_), channel_id=1, source_target_pairs={{0,3},{1,2},{2,1},{4,7},{5,6},{7,4},{8,11},{10,9},{11,8},{13,14},{... | collective-permute-start | bytes 786440 | tf_op jit(solution)/shard_map/ppermute | solution.py:421
  39.0 22.9 %collective-permute-start.10 = (f32[4,128,128]{2,1,0:T(8,128)}, f32[4,128,128]{2,1,0:T(8,128)S(1)}, u32[]{:S(2)}, u32[]{:S(2)}) collective-permute-start(f32[4,128,128]{2,1,0:T(8,128)} %get-tuple-element.32.refs_0_), channel_id=1, source_target_pairs={{0,2},{1,3},{3,1},{4,6},{5,7},{6,4},{9,11},{10,8},{11,9},{12,14},{... | collective-permute-start | bytes 786440 | tf_op jit(solution)/shard_map/ppermute | solution.py:421
  40.9 21.0 %collective-permute-start.9 = (f32[4,128,128]{2,1,0:T(8,128)S(1)}, f32[4,128,128]{2,1,0:T(8,128)S(1)}, u32[]{:S(2)}, u32[]{:S(2)}) collective-permute-start(f32[4,128,128]{2,1,0:T(8,128)S(1)} %collective-permute-done.5.refs_4_), channel_id=1, source_target_pairs={{0,24},{1,25},{2,26},{3,27},{4,28},{5,29},{6,30},{7,31},{8,16},{9,... | collective-permute-start | bytes 786440 | tf_op jit(solution)/shard_map/ppermute | solution.py:410
  43.3 18.7 %collective-permute-start.8 = (f32[4,128,128]{2,1,0:T(8,128)S(1)}, f32[4,128,128]{2,1,0:T(8,128)S(1)}, u32[]{:S(2)}, u32[]{:S(2)}) collective-permute-start(f32[4,128,128]{2,1,0:T(8,128)S(1)} %collective-permute-done.5.refs_4_), channel_id=1, source_target_pairs={{0,16},{1,17},{2,18},{3,19},{4,20},{5,21},{6,22},{7,23},{8,24},{9,... | collective-permute-start | bytes 786440 | tf_op jit(solution)/shard_map/ppermute | solution.py:410
  44.2 17.7 %collective-permute-start.7 = (f32[4,128,128]{2,1,0:T(8,128)S(1)}, f32[4,128,128]{2,1,0:T(8,128)S(1)}, u32[]{:S(2)}, u32[]{:S(2)}) collective-permute-start(f32[4,128,128]{2,1,0:T(8,128)S(1)} %collective-permute-done.5.refs_4_), channel_id=1, source_target_pairs={{0,8},{1,9},{2,10},{3,11},{4,12},{5,13},{6,14},{7,15},{8,0},{9,1},... | collective-permute-start | bytes 786440 | tf_op jit(solution)/shard_map/ppermute | solution.py:410
  62.0 5.0 %copy-start = (f32[1,1,36,128,128]{4,3,2,1,0:T(8,128)S(1)}, f32[1,1,36,128,128]{4,3,2,1,0:T(8,128)}, u32[]{:S(2)}) copy-start(f32[1,1,36,128,128]{4,3,2,1,0:T(8,128)} %param.3) | copy-start | bytes 7077892
  62.0 5.0 %copy-start.1 = (f32[4,128,128]{2,1,0:T(8,128)S(1)}, f32[4,128,128]{2,1,0:T(8,128)}, u32[]{:S(2)}) copy-start(f32[4,128,128]{2,1,0:T(8,128)} %get-tuple-element.32.refs_0_) | copy-start | bytes 786436
  62.0 5.0 %copy-start.2 = (s32[3,36]{1,0:T(4,128)S(1)}, s32[3,36]{1,0:T(4,128)}, u32[]{:S(2)}) copy-start(s32[3,36]{1,0:T(4,128)} %get-tuple-element.29.table) | copy-start | bytes 1300
  62.0 4.9 %collective-permute-start.13 = (f32[16,128,128]{2,1,0:T(8,128)S(1)}, f32[16,128,128]{2,1,0:T(8,128)S(1)}, u32[]{:S(2)}, u32[]{:S(2)}) collective-permute-start(f32[16,128,128]{2,1,0:T(8,128)S(1)} %pad_maximum_fusion), channel_id=1, source_target_pairs={{0,4},{1,5},{2,6},{3,7},{4,0},{5,1},{6,2},{7,3},{8,12},{9,13},{10,... | collective-permute-start | bytes 3145736 | tf_op jit(solution)/shard_map/ppermute | solution.py:410

commit v3 on v2

--- a/solution.py
+++ b/solution.py
@@ -9,6 +9,7 @@
 
 PANELS = 4
 FIRST = 3
+EARLY = 2
 GROUP = 32
 CHUNK = 16
 SUB = 8
@@ -285,43 +286,47 @@
     me = lax.axis_index("row")
     column = lax.axis_index("col")
 
-    load = pltpu.make_async_copy(values, slots_in, io_sems.at[0])
-    load.start()
+    def lanes_of(col):
+        return pl.ds(pl.multiple_of(jnp.minimum(col, PANELS - 1) * size, size), size)
+
     twice = (me ^ column) % col_devices == 0
     for p in range(col_devices):
         col = column ^ p
 
         @pl.when((col < PANELS) & jnp.logical_not(twice))
         def _():
-            lanes = pl.ds(pl.multiple_of(jnp.minimum(col, PANELS - 1) * size, size), size)
-            for place in range(count):
-                pltpu.make_async_copy(
-                    panels[p].at[place], raw.at[pl.ds(place * size, size), lanes], sems.at[0]
-                ).start()
+            target = raw.at[:own_rows, lanes_of(col)]
+            pltpu.make_async_copy(panels[p], target, sems.at[0]).start()
 
     for flip in range(row_devices):
         holder = me ^ flip
         group, col = holder // col_devices, spread(column, holder % col_devices)
+        if flip % 2 == 0:
+            source = near[flip // 2]
+        else:
+            source = across.at[flip // 2 * own_rows : (flip // 2 + 1) * own_rows]
+
+        @pl.when(twice & (col < PANELS) & (group == me // col_devices))
+        def _():
+            target = raw.at[:own_rows, lanes_of(col)]
+            pltpu.make_async_copy(source, target, sems.at[0]).start()
+
+    for flip in range(row_devices):
+        holder = me ^ flip
+        group, col = holder // col_devices, spread(column, holder % col_devices)
+        if flip % 2 == 0:
+            source = near[flip // 2]
+        else:
+            source = across.at[flip // 2 * own_rows : (flip // 2 + 1) * own_rows]
 
         @pl.when(col < PANELS)
         def _():
-            lanes = pl.ds(pl.multiple_of(jnp.minimum(col, PANELS - 1) * size, size), size)
-            for place in range(count):
-                if flip % 2 == 0:
-                    source = near[flip // 2].at[place]
-                else:
-                    source = across.at[flip // 2 * count + place]
-                start = pl.multiple_of(own_rows + (group * count + place) * size, size)
-                pltpu.make_async_copy(
-                    source, raw.at[pl.ds(start, size), lanes], sems.at[1]
-                ).start()
-
-                @pl.when(twice & (group == me // col_devices))
-                def _():
-                    pltpu.make_async_copy(
-                        source, raw.at[pl.ds(place * size, size), lanes], sems.at[0]
-                    ).start()
-
+            start = pl.multiple_of((group + 1) * own_rows, own_rows)
+            target = raw.at[pl.ds(start, own_rows), lanes_of(col)]
+            pltpu.make_async_copy(source, target, sems.at[1]).start()
+
+    load = pltpu.make_async_copy(values, slots_in, io_sems.at[0])
+    load.start()
     half = PANELS * size // 2
     for part in range(groups + 1):
         if part < 2:
@@ -347,7 +352,7 @@
                 product[place, start // size + side] = result[
                     place * size : (place + 1) * size, side * size : (side + 1) * size
                 ]
-    lanes = pl.ds(pl.multiple_of(jnp.minimum(column, PANELS - 1) * size, size), size)
+    lanes = lanes_of(column)
     for place in range(count):
         solved_block = raw[place * size : (place + 1) * size, lanes]
         if place == 0:
@@ -370,7 +375,7 @@
     slots, size, _ = values.shape
     col_devices, count = len(panels), panels[0].shape[0]
     groups = row_devices // col_devices
-    flat = [*panels, *near, across]
+    flat = [x.reshape(-1, size) for x in (*panels, *near, across)]
     width = PANELS * size
     rows = (groups + 1) * count * size
     return pl.pallas_call(
@@ -442,12 +447,16 @@
     panels = over_col(panel, lambda r, c: (r ^ c) % col_devices != 0)
 
     mine = jnp.concatenate(blocks, axis=0)
-    beside, turned, panels[1] = lax.optimization_barrier((send(mine, 2), turned, panels[1]))
+    beside, panels[EARLY], turned = lax.optimization_barrier(
+        (send(mine, 2), panels[EARLY], turned)
+    )
     near_lead = jnp.stack([mine, beside])
     across_lead = send(near_lead, 1)
     near = [turned if flip == 0 else send(turned, flip) for flip in range(0, row_devices, 2)]
     begun = factor_first(near_lead, across_lead)
-    near, panels[2:], begun = lax.optimization_barrier((near, panels[2:], begun))
+    late = [panels[p] for p in range(col_devices) if p != EARLY]
+    near, late, begun = lax.optimization_barrier((near, late, begun))
+    panels = late[:EARLY] + [panels[EARLY]] + late[EARLY:]
     across = send(jnp.concatenate(near, axis=0), 1)
     solved_lead = factor_second(*begun)
 

time: 75.2 us -> 73.5 us (0.977)
  waiting for transfers between devices: 24.7 us -> 19.9 us
  starting transfers between devices: 22.5 us -> 25.2 us
    ppermute x1, waiting for transfers between devices: 10.1 us -> 2.35 us  [body(): turned = lax.ppermute(panel, ('row', 'col'), pairs)]
    ppermute x6, waiting for transfers between devices: 10.9 us -> 13.9 us  [over_col(): got.append(lax.ppermute(x, ('row', 'col'), pairs))]
    ppermute x6, starting transfers between devices: 8.86 us -> 10.3 us  [over_col(): got.append(lax.ppermute(x, ('row', 'col'), pairs))]
  transfers between devices with their start and end apart: 14 -> 14, of which waited for: 6 -> 5; matrix products, arithmetic and copies ran while one was open for 0% -> 0% of each run, Pallas kernels for 22% -> 23%
where the time goes in v3:
time: 73.5 us; the launch traced here: 72 us
  Pallas kernels  26.4 us (36%)
  starting transfers between devices  25.2 us (34%)
  waiting for transfers between devices  19.9 us (27%)
    ppermute x6, waiting for transfers between devices, over_col(): got.append(lax.ppermute(x, ('row', 'col'), pairs))  13.9 us
    pallas_call x1, Pallas kernels, factor_first(): pl.pallas_call(first_kernel, name='factor_first', in_specs=[VMEM, VMEM],...  12.5 us
    ppermute x6, starting transfers between devices, over_col(): got.append(lax.ppermute(x, ('row', 'col'), pairs))  10.3 us
    ppermute x7, starting transfers between devices, send(): return lax.ppermute(x, ('row', 'col'), pairs)  9.1 us
    pallas_call x1, Pallas kernels, update(): pl.pallas_call(functools.partial(update_kernel, (row_devices, count, col_...  7.01 us
    ppermute x1, starting transfers between devices, body(): turned = lax.ppermute(panel, ('row', 'col'), pairs)  5.74 us
    pallas_call x1, Pallas kernels, factor_second(): pl.pallas_call(second_kernel, name='factor_second', in_specs=[VMEM, VMEM]...  4.06 us
    ppermute x7, waiting for transfers between devices, send(): return lax.ppermute(x, ('row', 'col'), pairs)  3.73 us
  transfers between devices with their start and end apart: 14, of which 5 were waited for; matrix products, arithmetic and copies ran while one was open for 0% of the time, Pallas kernels for 23%

profile of v3, /device:TPU:7, one launch (start us, length us, event | category | flops | bytes accessed | tf_op | source)
XLA Modules:
  0.0 72.0 jit_solution(1849532611821970981)
XLA Ops:
  0.0 2.7 %extract.1 = (f32[4,128,128]{2,1,0:T(8,128)}, f32[1,128,128]{2,1,0:T(8,128)}, s32[3,36]{1,0:T(4,128)}) custom-call(s32[2,36]{1,0:T(2,128)} %bitcast.31, s32[4,8]{1,0:T(4,128)} %bitcast.30, f32[36,128,128]{2,1,0:T(8,128)} %bitcast.17), custom_call_target="tpu_custom_call" | custom-call | tf_op jit(solution)/shard_map/extract/pallas_call | solution.py:70
  2.8 1.3 %collective-permute-start = (f32[1,128,128]{2,1,0:T(8,128)S(1)}, f32[1,128,128]{2,1,0:T(8,128)S(1)}, u32[]{:S(2)}, u32[]{:S(2)}) collective-permute-start(f32[1,128,128]{2,1,0:T(8,128)S(1)} %broadcast_select_fusion), channel_id=1, source_target_pairs={{0,16},{1,17},{2,18},{3,19},{4,20},{5,21},{6,22},{7,23},{8,24},{9,... | collective-permute-start | bytes 196616 | tf_op jit(solution)/shard_map/ppermute | solution.py:415
  4.1 3.7 %collective-permute-done = f32[1,128,128]{2,1,0:T(8,128)S(1)} collective-permute-done((f32[1,128,128]{2,1,0:T(8,128)S(1)}, f32[1,128,128]{2,1,0:T(8,128)S(1)}, u32[]{:S(2)}, u32[]{:S(2)}) %collective-permute-start) | collective-permute-done | bytes 65568 | tf_op jit(solution)/shard_map/ppermute | solution.py:415
  7.8 3.4 %collective-permute-start.3 = (f32[1,128,128]{2,1,0:T(8,128)S(1)}, f32[1,128,128]{2,1,0:T(8,128)S(1)}, u32[]{:S(2)}, u32[]{:S(2)}) collective-permute-start(f32[1,128,128]{2,1,0:T(8,128)S(1)} %fusion), channel_id=1, source_target_pairs={{0,3},{1,2},{2,1},{3,0},{4,7},{5,6},{6,5},{7,4},{8,11},{9,10},{10,... | collective-permute-start | bytes 196616 | tf_op jit(solution)/shard_map/ppermute | solution.py:426
  11.2 0.4 collective-permute-start.1
  11.5 1.3 %collective-permute-done.3 = f32[1,128,128]{2,1,0:T(8,128)S(1)} collective-permute-done((f32[1,128,128]{2,1,0:T(8,128)S(1)}, f32[1,128,128]{2,1,0:T(8,128)S(1)}, u32[]{:S(2)}, u32[]{:S(2)}) %collective-permute-start.3) | collective-permute-done | bytes 65568 | tf_op jit(solution)/shard_map/ppermute | solution.py:426
  12.8 3.8 %collective-permute-done.2 = f32[1,128,128]{2,1,0:T(8,128)S(1)} collective-permute-done((f32[1,128,128]{2,1,0:T(8,128)S(1)}, f32[1,128,128]{2,1,0:T(8,128)S(1)}, u32[]{:S(2)}, u32[]{:S(2)}) %collective-permute-start.2) | collective-permute-done | bytes 65568 | tf_op jit(solution)/shard_map/ppermute | solution.py:426
  16.7 0.3 collective-permute-start.4
  17.0 5.7 %collective-permute-start.6 = (f32[4,128,128]{2,1,0:T(8,128)}, f32[4,128,128]{2,1,0:T(8,128)S(1)}, u32[]{:S(2)}, u32[]{:S(2)}) collective-permute-start(f32[4,128,128]{2,1,0:T(8,128)} %get-tuple-element.42), channel_id=1, source_target_pairs={{0,0},{1,4},{2,8},{3,12},{4,9},{5,13},{6,1},{7,5},{8,2},{9,6},{10,... | collective-permute-start | bytes 786440 | tf_op jit(solution)/shard_map/ppermute | solution.py:445
  22.7 3.1 %collective-permute-start.5 = (f32[4,128,128]{2,1,0:T(8,128)}, f32[4,128,128]{2,1,0:T(8,128)S(1)}, u32[]{:S(2)}, u32[]{:S(2)}) collective-permute-start(f32[4,128,128]{2,1,0:T(8,128)} %get-tuple-element.42), channel_id=1, source_target_pairs={{0,2},{1,3},{3,1},{4,6},{5,7},{6,4},{9,11},{10,8},{11,9},{12,14},{... | collective-permute-start | bytes 786440 | tf_op jit(solution)/shard_map/ppermute | solution.py:426
  25.9 2.3 %collective-permute-done.6 = f32[4,128,128]{2,1,0:T(8,128)S(1)} collective-permute-done((f32[4,128,128]{2,1,0:T(8,128)}, f32[4,128,128]{2,1,0:T(8,128)S(1)}, u32[]{:S(2)}, u32[]{:S(2)}) %collective-permute-start.6) | collective-permute-done | bytes 262176 | tf_op jit(solution)/shard_map/ppermute | solution.py:445
  28.2 8.8 %collective-permute-done.5 = f32[4,128,128]{2,1,0:T(8,128)S(1)} collective-permute-done((f32[4,128,128]{2,1,0:T(8,128)}, f32[4,128,128]{2,1,0:T(8,128)S(1)}, u32[]{:S(2)}, u32[]{:S(2)}) %collective-permute-start.5) | collective-permute-done | bytes 262176 | tf_op jit(solution)/shard_map/ppermute | solution.py:426
  37.1 1.3 %collective-permute-start.12 = (f32[2,4,128,128]{3,2,1,0:T(8,128)S(1)}, f32[2,4,128,128]{3,2,1,0:T(8,128)S(1)}, u32[]{:S(2)}, u32[]{:S(2)}) collective-permute-start(f32[2,4,128,128]{3,2,1,0:T(8,128)S(1)} %pad_maximum_fusion.1.near), channel_id=1, source_target_pairs={{0,4},{1,5},{2,6},{3,7},{4,0},{5,1},{6,2},{7,3},{8,12},{9,13},{10,... | collective-permute-start | bytes 1572872 | tf_op jit(solution)/shard_map/ppermute | solution.py:415
  38.4 1.3 %collective-permute-start.11 = (f32[4,128,128]{2,1,0:T(8,128)}, f32[4,128,128]{2,1,0:T(8,128)S(1)}, u32[]{:S(2)}, u32[]{:S(2)}) collective-permute-start(f32[4,128,128]{2,1,0:T(8,128)} %get-tuple-element.42), channel_id=1, source_target_pairs={{0,3},{1,2},{2,1},{4,7},{5,6},{7,4},{8,11},{10,9},{11,8},{13,14},{... | collective-permute-start | bytes 786440 | tf_op jit(solution)/shard_map/ppermute | solution.py:426
  39.6 2.2 %collective-permute-start.10 = (f32[4,128,128]{2,1,0:T(8,128)}, f32[4,128,128]{2,1,0:T(8,128)S(1)}, u32[]{:S(2)}, u32[]{:S(2)}) collective-permute-start(f32[4,128,128]{2,1,0:T(8,128)} %get-tuple-element.42), channel_id=1, source_target_pairs={{0,1},{2,3},{3,2},{5,4},{6,7},{7,6},{8,9},{9,8},{10,11},{12,13},{1... | collective-permute-start | bytes 786440 | tf_op jit(solution)/shard_map/ppermute | solution.py:426
  41.8 1.5 %collective-permute-start.9 = (f32[4,128,128]{2,1,0:T(8,128)S(1)}, f32[4,128,128]{2,1,0:T(8,128)S(1)}, u32[]{:S(2)}, u32[]{:S(2)}) collective-permute-start(f32[4,128,128]{2,1,0:T(8,128)S(1)} %collective-permute-done.6), channel_id=1, source_target_pairs={{0,24},{1,25},{2,26},{3,27},{4,28},{5,29},{6,30},{7,31},{8,16},{9,... | collective-permute-start | bytes 786440 | tf_op jit(solution)/shard_map/ppermute | solution.py:415
  43.3 0.9 %collective-permute-start.8 = (f32[4,128,128]{2,1,0:T(8,128)S(1)}, f32[4,128,128]{2,1,0:T(8,128)S(1)}, u32[]{:S(2)}, u32[]{:S(2)}) collective-permute-start(f32[4,128,128]{2,1,0:T(8,128)S(1)} %collective-permute-done.6), channel_id=1, source_target_pairs={{0,16},{1,17},{2,18},{3,19},{4,20},{5,21},{6,22},{7,23},{8,24},{9,... | collective-permute-start | bytes 786440 | tf_op jit(solution)/shard_map/ppermute | solution.py:415
  44.2 0.4 collective-permute-start.7
  44.5 12.5 %factor_first.1 = (f32[10,128,128]{2,1,0:T(8,128)S(1)}, f32[6,128,128]{2,1,0:T(8,128)S(1)}) custom-call(f32[2,4,128,128]{3,2,1,0:T(8,128)S(1)} %pad_maximum_fusion.1.near, f32[2,4,128,128]{3,2,1,0:T(8,128)S(1)} %collective-permute-done.12.across), custom_call_target="tpu_custom_call" | custom-call | flops 8589934592 | bytes 16777216 | tf_op jit(solution)/shard_map/factor_first/pallas_call | solution.py:225
  57.2 0.1 pad_maximum_fusion
  57.2 0.0 copy-start
  57.3 3.5 %collective-permute-start.13 = (f32[16,128,128]{2,1,0:T(8,128)S(1)}, f32[16,128,128]{2,1,0:T(8,128)S(1)}, u32[]{:S(2)}, u32[]{:S(2)}) collective-permute-start(f32[16,128,128]{2,1,0:T(8,128)S(1)} %pad_maximum_fusion), channel_id=1, source_target_pairs={{0,4},{1,5},{2,6},{3,7},{4,0},{5,1},{6,2},{7,3},{8,12},{9,13},{10,... | collective-permute-start | bytes 3145736 | tf_op jit(solution)/shard_map/ppermute | solution.py:415
  60.7 4.1 %factor_second.1 = (f32[128,128]{1,0:T(8,128)S(1)}, bf16[512,512]{1,0:T(8,128)(2,1)S(1)}, bf16[512,512]{1,0:T(8,128)(2,1)S(1)}) custom-call(f32[10,128,128]{2,1,0:T(8,128)S(1)} %get-tuple-element.50.lead_in, f32[6,128,128]{2,1,0:T(8,128)S(1)} %get-tuple-element.51.inverse_in), custom_call_target="tpu_custom_call" | custom-call | flops 8589934592 | bytes 16777216 | tf_op jit(solution)/shard_map/factor_second/pallas_call | solution.py:243
  64.9 7.0 %update.1 = f32[36,128,128]{2,1,0:T(8,128)} custom-call(s32[3,36]{1,0:T(4,128)S(1)} %copy-done.2, f32[512,128]{1,0:T(8,128)S(1)} %bitcast.24, f32[512,128]{1,0:T(8,128)S(1)} %bitcast.27, f32[512,128]{1,0:T(8,128)S(1)} %bitcast.25, f32[512,128]{1,0:T(8,128)S(1)} %bitcast.26, f32[512,128]{1,0:T(8,128)S(1)} %bitcast.20, f32[512,128]{1,0:T(8,128)S(1)} %bitcast.23, ...), custom_call_target="tpu_custom_call" | custom-call | tf_op jit(solution)/shard_map/update/pallas_call | solution.py:381
  (22 shorter events, 0.1 us)
Async XLA Ops:
  2.8 5.0 %collective-permute-start = (f32[1,128,128]{2,1,0:T(8,128)S(1)}, f32[1,128,128]{2,1,0:T(8,128)S(1)}, u32[]{:S(2)}, u32[]{:S(2)}) collective-permute-start(f32[1,128,128]{2,1,0:T(8,128)S(1)} %broadcast_select_fusion), channel_id=1, source_target_pairs={{0,16},{1,17},{2,18},{3,19},{4,20},{5,21},{6,22},{7,23},{8,24},{9,... | collective-permute-start | bytes 196616 | tf_op jit(solution)/shard_map/ppermute | solution.py:415
  7.8 5.0 %collective-permute-start.3 = (f32[1,128,128]{2,1,0:T(8,128)S(1)}, f32[1,128,128]{2,1,0:T(8,128)S(1)}, u32[]{:S(2)}, u32[]{:S(2)}) collective-permute-start(f32[1,128,128]{2,1,0:T(8,128)S(1)} %fusion), channel_id=1, source_target_pairs={{0,3},{1,2},{2,1},{3,0},{4,7},{5,6},{6,5},{7,4},{8,11},{9,10},{10,... | collective-permute-start | bytes 196616 | tf_op jit(solution)/shard_map/ppermute | solution.py:426
  11.2 5.4 %collective-permute-start.2 = (f32[1,128,128]{2,1,0:T(8,128)S(1)}, f32[1,128,128]{2,1,0:T(8,128)S(1)}, u32[]{:S(2)}, u32[]{:S(2)}) collective-permute-start(f32[1,128,128]{2,1,0:T(8,128)S(1)} %fusion), channel_id=1, source_target_pairs={{0,2},{1,3},{2,0},{3,1},{4,6},{5,7},{6,4},{7,5},{8,10},{9,11},{10,... | collective-permute-start | bytes 196616 | tf_op jit(solution)/shard_map/ppermute | solution.py:426
  11.2 5.4 %collective-permute-start.1 = (f32[1,128,128]{2,1,0:T(8,128)S(1)}, f32[1,128,128]{2,1,0:T(8,128)S(1)}, u32[]{:S(2)}, u32[]{:S(2)}) collective-permute-start(f32[1,128,128]{2,1,0:T(8,128)S(1)} %fusion), channel_id=1, source_target_pairs={{0,1},{1,0},{2,3},{3,2},{4,5},{5,4},{6,7},{7,6},{8,9},{9,8},{10,11... | collective-permute-start | bytes 196616 | tf_op jit(solution)/shard_map/ppermute | solution.py:426
  16.7 9.2 %collective-permute-start.4 = (f32[4,128,128]{2,1,0:T(8,128)S(1)}, f32[4,128,128]{2,1,0:T(8,128)S(1)}, u32[]{:S(2)}, u32[]{:S(2)}) collective-permute-start(f32[4,128,128]{2,1,0:T(8,128)S(1)} %constant_dynamic-update-slice_fusion), channel_id=1, source_target_pairs={{0,8},{1,9},{2,10},{3,11},{4,12},{5,13},{6,14},{7,15},{8,0},{9,1},... | collective-permute-start | bytes 786440 | tf_op jit(solution)/shard_map/ppermute | solution.py:415
  17.0 11.2 %collective-permute-start.6 = (f32[4,128,128]{2,1,0:T(8,128)}, f32[4,128,128]{2,1,0:T(8,128)S(1)}, u32[]{:S(2)}, u32[]{:S(2)}) collective-permute-start(f32[4,128,128]{2,1,0:T(8,128)} %get-tuple-element.42), channel_id=1, source_target_pairs={{0,0},{1,4},{2,8},{3,12},{4,9},{5,13},{6,1},{7,5},{8,2},{9,6},{10,... | collective-permute-start | bytes 786440 | tf_op jit(solution)/shard_map/ppermute | solution.py:445
  22.7 14.3 %collective-permute-start.5 = (f32[4,128,128]{2,1,0:T(8,128)}, f32[4,128,128]{2,1,0:T(8,128)S(1)}, u32[]{:S(2)}, u32[]{:S(2)}) collective-permute-start(f32[4,128,128]{2,1,0:T(8,128)} %get-tuple-element.42), channel_id=1, source_target_pairs={{0,2},{1,3},{3,1},{4,6},{5,7},{6,4},{9,11},{10,8},{11,9},{12,14},{... | collective-permute-start | bytes 786440 | tf_op jit(solution)/shard_map/ppermute | solution.py:426
  37.1 7.1 %collective-permute-start.12 = (f32[2,4,128,128]{3,2,1,0:T(8,128)S(1)}, f32[2,4,128,128]{3,2,1,0:T(8,128)S(1)}, u32[]{:S(2)}, u32[]{:S(2)}) collective-permute-start(f32[2,4,128,128]{3,2,1,0:T(8,128)S(1)} %pad_maximum_fusion.1.near), channel_id=1, source_target_pairs={{0,4},{1,5},{2,6},{3,7},{4,0},{5,1},{6,2},{7,3},{8,12},{9,13},{10,... | collective-permute-start | bytes 1572872 | tf_op jit(solution)/shard_map/ppermute | solution.py:415
  38.4 18.7 %collective-permute-start.11 = (f32[4,128,128]{2,1,0:T(8,128)}, f32[4,128,128]{2,1,0:T(8,128)S(1)}, u32[]{:S(2)}, u32[]{:S(2)}) collective-permute-start(f32[4,128,128]{2,1,0:T(8,128)} %get-tuple-element.42), channel_id=1, source_target_pairs={{0,3},{1,2},{2,1},{4,7},{5,6},{7,4},{8,11},{10,9},{11,8},{13,14},{... | collective-permute-start | bytes 786440 | tf_op jit(solution)/shard_map/ppermute | solution.py:426
  39.6 17.5 %collective-permute-start.10 = (f32[4,128,128]{2,1,0:T(8,128)}, f32[4,128,128]{2,1,0:T(8,128)S(1)}, u32[]{:S(2)}, u32[]{:S(2)}) collective-permute-start(f32[4,128,128]{2,1,0:T(8,128)} %get-tuple-element.42), channel_id=1, source_target_pairs={{0,1},{2,3},{3,2},{5,4},{6,7},{7,6},{8,9},{9,8},{10,11},{12,13},{1... | collective-permute-start | bytes 786440 | tf_op jit(solution)/shard_map/ppermute | solution.py:426
  41.8 15.3 %collective-permute-start.9 = (f32[4,128,128]{2,1,0:T(8,128)S(1)}, f32[4,128,128]{2,1,0:T(8,128)S(1)}, u32[]{:S(2)}, u32[]{:S(2)}) collective-permute-start(f32[4,128,128]{2,1,0:T(8,128)S(1)} %collective-permute-done.6), channel_id=1, source_target_pairs={{0,24},{1,25},{2,26},{3,27},{4,28},{5,29},{6,30},{7,31},{8,16},{9,... | collective-permute-start | bytes 786440 | tf_op jit(solution)/shard_map/ppermute | solution.py:415
  43.3 13.8 %collective-permute-start.8 = (f32[4,128,128]{2,1,0:T(8,128)S(1)}, f32[4,128,128]{2,1,0:T(8,128)S(1)}, u32[]{:S(2)}, u32[]{:S(2)}) collective-permute-start(f32[4,128,128]{2,1,0:T(8,128)S(1)} %collective-permute-done.6), channel_id=1, source_target_pairs={{0,16},{1,17},{2,18},{3,19},{4,20},{5,21},{6,22},{7,23},{8,24},{9,... | collective-permute-start | bytes 786440 | tf_op jit(solution)/shard_map/ppermute | solution.py:415
  44.2 13.0 %collective-permute-start.7 = (f32[4,128,128]{2,1,0:T(8,128)S(1)}, f32[4,128,128]{2,1,0:T(8,128)S(1)}, u32[]{:S(2)}, u32[]{:S(2)}) collective-permute-start(f32[4,128,128]{2,1,0:T(8,128)S(1)} %collective-permute-done.6), channel_id=1, source_target_pairs={{0,8},{1,9},{2,10},{3,11},{4,12},{5,13},{6,14},{7,15},{8,0},{9,1},... | collective-permute-start | bytes 786440 | tf_op jit(solution)/shard_map/ppermute | solution.py:415
  57.2 7.6 %copy-start = (f32[1,1,36,128,128]{4,3,2,1,0:T(8,128)S(1)}, f32[1,1,36,128,128]{4,3,2,1,0:T(8,128)}, u32[]{:S(2)}) copy-start(f32[1,1,36,128,128]{4,3,2,1,0:T(8,128)} %param.3) | copy-start | bytes 7077892
  57.2 7.6 %copy-start.1 = (f32[4,128,128]{2,1,0:T(8,128)S(1)}, f32[4,128,128]{2,1,0:T(8,128)}, u32[]{:S(2)}) copy-start(f32[4,128,128]{2,1,0:T(8,128)} %get-tuple-element.42) | copy-start | bytes 786436
  57.3 7.6 %copy-start.2 = (s32[3,36]{1,0:T(4,128)S(1)}, s32[3,36]{1,0:T(4,128)}, u32[]{:S(2)}) copy-start(s32[3,36]{1,0:T(4,128)} %get-tuple-element.30.table) | copy-start | bytes 1300
  57.3 7.5 %collective-permute-start.13 = (f32[16,128,128]{2,1,0:T(8,128)S(1)}, f32[16,128,128]{2,1,0:T(8,128)S(1)}, u32[]{:S(2)}, u32[]{:S(2)}) collective-permute-start(f32[16,128,128]{2,1,0:T(8,128)S(1)} %pad_maximum_fusion), channel_id=1, source_target_pairs={{0,4},{1,5},{2,6},{3,7},{4,0},{5,1},{6,2},{7,3},{8,12},{9,13},{10,... | collective-permute-start | bytes 3145736 | tf_op jit(solution)/shard_map/ppermute | solution.py:415

commit v4 on v3

--- a/solution.py
+++ b/solution.py
@@ -447,8 +447,8 @@
     panels = over_col(panel, lambda r, c: (r ^ c) % col_devices != 0)
 
     mine = jnp.concatenate(blocks, axis=0)
-    beside, panels[EARLY], turned = lax.optimization_barrier(
-        (send(mine, 2), panels[EARLY], turned)
+    panels[EARLY], beside, turned = lax.optimization_barrier(
+        (panels[EARLY], send(mine, 2), turned)
     )
     near_lead = jnp.stack([mine, beside])
     across_lead = send(near_lead, 1)

time: 73.5 us -> 73.5 us (level)
  no operation moved by 1% of the time
where the time goes in v4:
time: 73.5 us; the launch traced here: 72 us
  Pallas kernels  26.4 us (36%)
  starting transfers between devices  25.2 us (34%)
  waiting for transfers between devices  19.9 us (27%)
    ppermute x6, waiting for transfers between devices, over_col(): got.append(lax.ppermute(x, ('row', 'col'), pairs))  13.9 us
    pallas_call x1, Pallas kernels, factor_first(): pl.pallas_call(first_kernel, name='factor_first', in_specs=[VMEM, VMEM],...  12.5 us
    ppermute x6, starting transfers between devices, over_col(): got.append(lax.ppermute(x, ('row', 'col'), pairs))  10.3 us
    ppermute x7, starting transfers between devices, send(): return lax.ppermute(x, ('row', 'col'), pairs)  9.1 us
    pallas_call x1, Pallas kernels, update(): pl.pallas_call(functools.partial(update_kernel, (row_devices, count, col_...  7.01 us
    ppermute x1, starting transfers between devices, body(): turned = lax.ppermute(panel, ('row', 'col'), pairs)  5.74 us
    pallas_call x1, Pallas kernels, factor_second(): pl.pallas_call(second_kernel, name='factor_second', in_specs=[VMEM, VMEM]...  4.06 us
    ppermute x7, waiting for transfers between devices, send(): return lax.ppermute(x, ('row', 'col'), pairs)  3.73 us
  transfers between devices with their start and end apart: 14, of which 5 were waited for; matrix products, arithmetic and copies ran while one was open for 0% of the time, Pallas kernels for 23%

profile of v4, /device:TPU:7, one launch (start us, length us, event | category | flops | bytes accessed | tf_op | source)
XLA Modules:
  0.0 72.0 jit_solution(1849532611821970981)
XLA Ops:
  0.0 2.7 %extract.1 = (f32[4,128,128]{2,1,0:T(8,128)}, f32[1,128,128]{2,1,0:T(8,128)}, s32[3,36]{1,0:T(4,128)}) custom-call(s32[2,36]{1,0:T(2,128)} %bitcast.31, s32[4,8]{1,0:T(4,128)} %bitcast.30, f32[36,128,128]{2,1,0:T(8,128)} %bitcast.17), custom_call_target="tpu_custom_call" | custom-call | tf_op jit(solution)/shard_map/extract/pallas_call | solution.py:70
  2.8 1.3 %collective-permute-start = (f32[1,128,128]{2,1,0:T(8,128)S(1)}, f32[1,128,128]{2,1,0:T(8,128)S(1)}, u32[]{:S(2)}, u32[]{:S(2)}) collective-permute-start(f32[1,128,128]{2,1,0:T(8,128)S(1)} %broadcast_select_fusion), channel_id=1, source_target_pairs={{0,16},{1,17},{2,18},{3,19},{4,20},{5,21},{6,22},{7,23},{8,24},{9,... | collective-permute-start | bytes 196616 | tf_op jit(solution)/shard_map/ppermute | solution.py:415
  4.1 3.7 %collective-permute-done = f32[1,128,128]{2,1,0:T(8,128)S(1)} collective-permute-done((f32[1,128,128]{2,1,0:T(8,128)S(1)}, f32[1,128,128]{2,1,0:T(8,128)S(1)}, u32[]{:S(2)}, u32[]{:S(2)}) %collective-permute-start) | collective-permute-done | bytes 65568 | tf_op jit(solution)/shard_map/ppermute | solution.py:415
  7.8 3.4 %collective-permute-start.3 = (f32[1,128,128]{2,1,0:T(8,128)S(1)}, f32[1,128,128]{2,1,0:T(8,128)S(1)}, u32[]{:S(2)}, u32[]{:S(2)}) collective-permute-start(f32[1,128,128]{2,1,0:T(8,128)S(1)} %fusion), channel_id=1, source_target_pairs={{0,3},{1,2},{2,1},{3,0},{4,7},{5,6},{6,5},{7,4},{8,11},{9,10},{10,... | collective-permute-start | bytes 196616 | tf_op jit(solution)/shard_map/ppermute | solution.py:426
  11.2 0.4 collective-permute-start.1
  11.5 1.3 %collective-permute-done.3 = f32[1,128,128]{2,1,0:T(8,128)S(1)} collective-permute-done((f32[1,128,128]{2,1,0:T(8,128)S(1)}, f32[1,128,128]{2,1,0:T(8,128)S(1)}, u32[]{:S(2)}, u32[]{:S(2)}) %collective-permute-start.3) | collective-permute-done | bytes 65568 | tf_op jit(solution)/shard_map/ppermute | solution.py:426
  12.8 3.8 %collective-permute-done.2 = f32[1,128,128]{2,1,0:T(8,128)S(1)} collective-permute-done((f32[1,128,128]{2,1,0:T(8,128)S(1)}, f32[1,128,128]{2,1,0:T(8,128)S(1)}, u32[]{:S(2)}, u32[]{:S(2)}) %collective-permute-start.2) | collective-permute-done | bytes 65568 | tf_op jit(solution)/shard_map/ppermute | solution.py:426
  16.7 0.3 collective-permute-start.5
  17.0 5.7 %collective-permute-start.6 = (f32[4,128,128]{2,1,0:T(8,128)}, f32[4,128,128]{2,1,0:T(8,128)S(1)}, u32[]{:S(2)}, u32[]{:S(2)}) collective-permute-start(f32[4,128,128]{2,1,0:T(8,128)} %get-tuple-element.42), channel_id=1, source_target_pairs={{0,0},{1,4},{2,8},{3,12},{4,9},{5,13},{6,1},{7,5},{8,2},{9,6},{10,... | collective-permute-start | bytes 786440 | tf_op jit(solution)/shard_map/ppermute | solution.py:445
  22.7 3.1 %collective-permute-start.4 = (f32[4,128,128]{2,1,0:T(8,128)}, f32[4,128,128]{2,1,0:T(8,128)S(1)}, u32[]{:S(2)}, u32[]{:S(2)}) collective-permute-start(f32[4,128,128]{2,1,0:T(8,128)} %get-tuple-element.42), channel_id=1, source_target_pairs={{0,2},{1,3},{3,1},{4,6},{5,7},{6,4},{9,11},{10,8},{11,9},{12,14},{... | collective-permute-start | bytes 786440 | tf_op jit(solution)/shard_map/ppermute | solution.py:426
  25.9 2.3 %collective-permute-done.6 = f32[4,128,128]{2,1,0:T(8,128)S(1)} collective-permute-done((f32[4,128,128]{2,1,0:T(8,128)}, f32[4,128,128]{2,1,0:T(8,128)S(1)}, u32[]{:S(2)}, u32[]{:S(2)}) %collective-permute-start.6) | collective-permute-done | bytes 262176 | tf_op jit(solution)/shard_map/ppermute | solution.py:445
  28.2 8.8 %collective-permute-done.4 = f32[4,128,128]{2,1,0:T(8,128)S(1)} collective-permute-done((f32[4,128,128]{2,1,0:T(8,128)}, f32[4,128,128]{2,1,0:T(8,128)S(1)}, u32[]{:S(2)}, u32[]{:S(2)}) %collective-permute-start.4) | collective-permute-done | bytes 262176 | tf_op jit(solution)/shard_map/ppermute | solution.py:426
  37.1 1.3 %collective-permute-start.12 = (f32[2,4,128,128]{3,2,1,0:T(8,128)S(1)}, f32[2,4,128,128]{3,2,1,0:T(8,128)S(1)}, u32[]{:S(2)}, u32[]{:S(2)}) collective-permute-start(f32[2,4,128,128]{3,2,1,0:T(8,128)S(1)} %pad_maximum_fusion.1.near), channel_id=1, source_target_pairs={{0,4},{1,5},{2,6},{3,7},{4,0},{5,1},{6,2},{7,3},{8,12},{9,13},{10,... | collective-permute-start | bytes 1572872 | tf_op jit(solution)/shard_map/ppermute | solution.py:415
  38.4 1.3 %collective-permute-start.11 = (f32[4,128,128]{2,1,0:T(8,128)}, f32[4,128,128]{2,1,0:T(8,128)S(1)}, u32[]{:S(2)}, u32[]{:S(2)}) collective-permute-start(f32[4,128,128]{2,1,0:T(8,128)} %get-tuple-element.42), channel_id=1, source_target_pairs={{0,3},{1,2},{2,1},{4,7},{5,6},{7,4},{8,11},{10,9},{11,8},{13,14},{... | collective-permute-start | bytes 786440 | tf_op jit(solution)/shard_map/ppermute | solution.py:426
  39.6 2.2 %collective-permute-start.10 = (f32[4,128,128]{2,1,0:T(8,128)}, f32[4,128,128]{2,1,0:T(8,128)S(1)}, u32[]{:S(2)}, u32[]{:S(2)}) collective-permute-start(f32[4,128,128]{2,1,0:T(8,128)} %get-tuple-element.42), channel_id=1, source_target_pairs={{0,1},{2,3},{3,2},{5,4},{6,7},{7,6},{8,9},{9,8},{10,11},{12,13},{1... | collective-permute-start | bytes 786440 | tf_op jit(solution)/shard_map/ppermute | solution.py:426
  41.8 1.5 %collective-permute-start.9 = (f32[4,128,128]{2,1,0:T(8,128)S(1)}, f32[4,128,128]{2,1,0:T(8,128)S(1)}, u32[]{:S(2)}, u32[]{:S(2)}) collective-permute-start(f32[4,128,128]{2,1,0:T(8,128)S(1)} %collective-permute-done.6), channel_id=1, source_target_pairs={{0,24},{1,25},{2,26},{3,27},{4,28},{5,29},{6,30},{7,31},{8,16},{9,... | collective-permute-start | bytes 786440 | tf_op jit(solution)/shard_map/ppermute | solution.py:415
  43.3 0.9 %collective-permute-start.8 = (f32[4,128,128]{2,1,0:T(8,128)S(1)}, f32[4,128,128]{2,1,0:T(8,128)S(1)}, u32[]{:S(2)}, u32[]{:S(2)}) collective-permute-start(f32[4,128,128]{2,1,0:T(8,128)S(1)} %collective-permute-done.6), channel_id=1, source_target_pairs={{0,16},{1,17},{2,18},{3,19},{4,20},{5,21},{6,22},{7,23},{8,24},{9,... | collective-permute-start | bytes 786440 | tf_op jit(solution)/shard_map/ppermute | solution.py:415
  44.2 0.4 collective-permute-start.7
  44.5 12.5 %factor_first.1 = (f32[10,128,128]{2,1,0:T(8,128)S(1)}, f32[6,128,128]{2,1,0:T(8,128)S(1)}) custom-call(f32[2,4,128,128]{3,2,1,0:T(8,128)S(1)} %pad_maximum_fusion.1.near, f32[2,4,128,128]{3,2,1,0:T(8,128)S(1)} %collective-permute-done.12.across), custom_call_target="tpu_custom_call" | custom-call | flops 8589934592 | bytes 16777216 | tf_op jit(solution)/shard_map/factor_first/pallas_call | solution.py:225
  57.2 0.1 pad_maximum_fusion
  57.2 0.0 copy-start
  57.3 3.5 %collective-permute-start.13 = (f32[16,128,128]{2,1,0:T(8,128)S(1)}, f32[16,128,128]{2,1,0:T(8,128)S(1)}, u32[]{:S(2)}, u32[]{:S(2)}) collective-permute-start(f32[16,128,128]{2,1,0:T(8,128)S(1)} %pad_maximum_fusion), channel_id=1, source_target_pairs={{0,4},{1,5},{2,6},{3,7},{4,0},{5,1},{6,2},{7,3},{8,12},{9,13},{10,... | collective-permute-start | bytes 3145736 | tf_op jit(solution)/shard_map/ppermute | solution.py:415
  60.7 4.1 %factor_second.1 = (f32[128,128]{1,0:T(8,128)S(1)}, bf16[512,512]{1,0:T(8,128)(2,1)S(1)}, bf16[512,512]{1,0:T(8,128)(2,1)S(1)}) custom-call(f32[10,128,128]{2,1,0:T(8,128)S(1)} %get-tuple-element.50.lead_in, f32[6,128,128]{2,1,0:T(8,128)S(1)} %get-tuple-element.51.inverse_in), custom_call_target="tpu_custom_call" | custom-call | flops 8589934592 | bytes 16777216 | tf_op jit(solution)/shard_map/factor_second/pallas_call | solution.py:243
  64.9 7.0 %update.1 = f32[36,128,128]{2,1,0:T(8,128)} custom-call(s32[3,36]{1,0:T(4,128)S(1)} %copy-done.2, f32[512,128]{1,0:T(8,128)S(1)} %bitcast.24, f32[512,128]{1,0:T(8,128)S(1)} %bitcast.27, f32[512,128]{1,0:T(8,128)S(1)} %bitcast.25, f32[512,128]{1,0:T(8,128)S(1)} %bitcast.26, f32[512,128]{1,0:T(8,128)S(1)} %bitcast.20, f32[512,128]{1,0:T(8,128)S(1)} %bitcast.23, ...), custom_call_target="tpu_custom_call" | custom-call | tf_op jit(solution)/shard_map/update/pallas_call | solution.py:381
  (22 shorter events, 0.1 us)
Async XLA Ops:
  2.8 5.0 %collective-permute-start = (f32[1,128,128]{2,1,0:T(8,128)S(1)}, f32[1,128,128]{2,1,0:T(8,128)S(1)}, u32[]{:S(2)}, u32[]{:S(2)}) collective-permute-start(f32[1,128,128]{2,1,0:T(8,128)S(1)} %broadcast_select_fusion), channel_id=1, source_target_pairs={{0,16},{1,17},{2,18},{3,19},{4,20},{5,21},{6,22},{7,23},{8,24},{9,... | collective-permute-start | bytes 196616 | tf_op jit(solution)/shard_map/ppermute | solution.py:415
  7.8 5.0 %collective-permute-start.3 = (f32[1,128,128]{2,1,0:T(8,128)S(1)}, f32[1,128,128]{2,1,0:T(8,128)S(1)}, u32[]{:S(2)}, u32[]{:S(2)}) collective-permute-start(f32[1,128,128]{2,1,0:T(8,128)S(1)} %fusion), channel_id=1, source_target_pairs={{0,3},{1,2},{2,1},{3,0},{4,7},{5,6},{6,5},{7,4},{8,11},{9,10},{10,... | collective-permute-start | bytes 196616 | tf_op jit(solution)/shard_map/ppermute | solution.py:426
  11.2 5.4 %collective-permute-start.2 = (f32[1,128,128]{2,1,0:T(8,128)S(1)}, f32[1,128,128]{2,1,0:T(8,128)S(1)}, u32[]{:S(2)}, u32[]{:S(2)}) collective-permute-start(f32[1,128,128]{2,1,0:T(8,128)S(1)} %fusion), channel_id=1, source_target_pairs={{0,2},{1,3},{2,0},{3,1},{4,6},{5,7},{6,4},{7,5},{8,10},{9,11},{10,... | collective-permute-start | bytes 196616 | tf_op jit(solution)/shard_map/ppermute | solution.py:426
  11.2 5.4 %collective-permute-start.1 = (f32[1,128,128]{2,1,0:T(8,128)S(1)}, f32[1,128,128]{2,1,0:T(8,128)S(1)}, u32[]{:S(2)}, u32[]{:S(2)}) collective-permute-start(f32[1,128,128]{2,1,0:T(8,128)S(1)} %fusion), channel_id=1, source_target_pairs={{0,1},{1,0},{2,3},{3,2},{4,5},{5,4},{6,7},{7,6},{8,9},{9,8},{10,11... | collective-permute-start | bytes 196616 | tf_op jit(solution)/shard_map/ppermute | solution.py:426
  16.7 9.2 %collective-permute-start.5 = (f32[4,128,128]{2,1,0:T(8,128)S(1)}, f32[4,128,128]{2,1,0:T(8,128)S(1)}, u32[]{:S(2)}, u32[]{:S(2)}) collective-permute-start(f32[4,128,128]{2,1,0:T(8,128)S(1)} %constant_dynamic-update-slice_fusion), channel_id=1, source_target_pairs={{0,8},{1,9},{2,10},{3,11},{4,12},{5,13},{6,14},{7,15},{8,0},{9,1},... | collective-permute-start | bytes 786440 | tf_op jit(solution)/shard_map/ppermute | solution.py:415
  17.0 11.2 %collective-permute-start.6 = (f32[4,128,128]{2,1,0:T(8,128)}, f32[4,128,128]{2,1,0:T(8,128)S(1)}, u32[]{:S(2)}, u32[]{:S(2)}) collective-permute-start(f32[4,128,128]{2,1,0:T(8,128)} %get-tuple-element.42), channel_id=1, source_target_pairs={{0,0},{1,4},{2,8},{3,12},{4,9},{5,13},{6,1},{7,5},{8,2},{9,6},{10,... | collective-permute-start | bytes 786440 | tf_op jit(solution)/shard_map/ppermute | solution.py:445
  22.7 14.3 %collective-permute-start.4 = (f32[4,128,128]{2,1,0:T(8,128)}, f32[4,128,128]{2,1,0:T(8,128)S(1)}, u32[]{:S(2)}, u32[]{:S(2)}) collective-permute-start(f32[4,128,128]{2,1,0:T(8,128)} %get-tuple-element.42), channel_id=1, source_target_pairs={{0,2},{1,3},{3,1},{4,6},{5,7},{6,4},{9,11},{10,8},{11,9},{12,14},{... | collective-permute-start | bytes 786440 | tf_op jit(solution)/shard_map/ppermute | solution.py:426
  37.1 7.1 %collective-permute-start.12 = (f32[2,4,128,128]{3,2,1,0:T(8,128)S(1)}, f32[2,4,128,128]{3,2,1,0:T(8,128)S(1)}, u32[]{:S(2)}, u32[]{:S(2)}) collective-permute-start(f32[2,4,128,128]{3,2,1,0:T(8,128)S(1)} %pad_maximum_fusion.1.near), channel_id=1, source_target_pairs={{0,4},{1,5},{2,6},{3,7},{4,0},{5,1},{6,2},{7,3},{8,12},{9,13},{10,... | collective-permute-start | bytes 1572872 | tf_op jit(solution)/shard_map/ppermute | solution.py:415
  38.4 18.7 %collective-permute-start.11 = (f32[4,128,128]{2,1,0:T(8,128)}, f32[4,128,128]{2,1,0:T(8,128)S(1)}, u32[]{:S(2)}, u32[]{:S(2)}) collective-permute-start(f32[4,128,128]{2,1,0:T(8,128)} %get-tuple-element.42), channel_id=1, source_target_pairs={{0,3},{1,2},{2,1},{4,7},{5,6},{7,4},{8,11},{10,9},{11,8},{13,14},{... | collective-permute-start | bytes 786440 | tf_op jit(solution)/shard_map/ppermute | solution.py:426
  39.6 17.5 %collective-permute-start.10 = (f32[4,128,128]{2,1,0:T(8,128)}, f32[4,128,128]{2,1,0:T(8,128)S(1)}, u32[]{:S(2)}, u32[]{:S(2)}) collective-permute-start(f32[4,128,128]{2,1,0:T(8,128)} %get-tuple-element.42), channel_id=1, source_target_pairs={{0,1},{2,3},{3,2},{5,4},{6,7},{7,6},{8,9},{9,8},{10,11},{12,13},{1... | collective-permute-start | bytes 786440 | tf_op jit(solution)/shard_map/ppermute | solution.py:426
  41.8 15.3 %collective-permute-start.9 = (f32[4,128,128]{2,1,0:T(8,128)S(1)}, f32[4,128,128]{2,1,0:T(8,128)S(1)}, u32[]{:S(2)}, u32[]{:S(2)}) collective-permute-start(f32[4,128,128]{2,1,0:T(8,128)S(1)} %collective-permute-done.6), channel_id=1, source_target_pairs={{0,24},{1,25},{2,26},{3,27},{4,28},{5,29},{6,30},{7,31},{8,16},{9,... | collective-permute-start | bytes 786440 | tf_op jit(solution)/shard_map/ppermute | solution.py:415
  43.3 13.8 %collective-permute-start.8 = (f32[4,128,128]{2,1,0:T(8,128)S(1)}, f32[4,128,128]{2,1,0:T(8,128)S(1)}, u32[]{:S(2)}, u32[]{:S(2)}) collective-permute-start(f32[4,128,128]{2,1,0:T(8,128)S(1)} %collective-permute-done.6), channel_id=1, source_target_pairs={{0,16},{1,17},{2,18},{3,19},{4,20},{5,21},{6,22},{7,23},{8,24},{9,... | collective-permute-start | bytes 786440 | tf_op jit(solution)/shard_map/ppermute | solution.py:415
  44.2 13.0 %collective-permute-start.7 = (f32[4,128,128]{2,1,0:T(8,128)S(1)}, f32[4,128,128]{2,1,0:T(8,128)S(1)}, u32[]{:S(2)}, u32[]{:S(2)}) collective-permute-start(f32[4,128,128]{2,1,0:T(8,128)S(1)} %collective-permute-done.6), channel_id=1, source_target_pairs={{0,8},{1,9},{2,10},{3,11},{4,12},{5,13},{6,14},{7,15},{8,0},{9,1},... | collective-permute-start | bytes 786440 | tf_op jit(solution)/shard_map/ppermute | solution.py:415
  57.2 7.6 %copy-start = (f32[1,1,36,128,128]{4,3,2,1,0:T(8,128)S(1)}, f32[1,1,36,128,128]{4,3,2,1,0:T(8,128)}, u32[]{:S(2)}) copy-start(f32[1,1,36,128,128]{4,3,2,1,0:T(8,128)} %param.3) | copy-start | bytes 7077892
  57.2 7.6 %copy-start.1 = (f32[4,128,128]{2,1,0:T(8,128)S(1)}, f32[4,128,128]{2,1,0:T(8,128)}, u32[]{:S(2)}) copy-start(f32[4,128,128]{2,1,0:T(8,128)} %get-tuple-element.42) | copy-start | bytes 786436
  57.3 7.6 %copy-start.2 = (s32[3,36]{1,0:T(4,128)S(1)}, s32[3,36]{1,0:T(4,128)}, u32[]{:S(2)}) copy-start(s32[3,36]{1,0:T(4,128)} %get-tuple-element.30.table) | copy-start | bytes 1300
  57.3 7.5 %collective-permute-start.13 = (f32[16,128,128]{2,1,0:T(8,128)S(1)}, f32[16,128,128]{2,1,0:T(8,128)S(1)}, u32[]{:S(2)}, u32[]{:S(2)}) collective-permute-start(f32[16,128,128]{2,1,0:T(8,128)S(1)} %pad_maximum_fusion), channel_id=1, source_target_pairs={{0,4},{1,5},{2,6},{3,7},{4,0},{5,1},{6,2},{7,3},{8,12},{9,13},{10,... | collective-permute-start | bytes 3145736 | tf_op jit(solution)/shard_map/ppermute | solution.py:415
